TPU v7x, 512 devices: a whole 4x8x8 slice. The times are simulated.
512 devices in a mesh: sta: 32 (over x, z), seg: 8 (over y), band: 2 (over core).
Axes of the slice: x: 4, y: 8, z: 8, core: 2. Of those that a mesh axis runs over, the one named last changes fastest.
Arguments:
- raw_spectra: bfloat16 [8, 8192, 2, 8192], P('seg', 'sta', None, 'band'), may hold values from -200 to 200
- pair_list: int32 [96, 2], P('sta'), may hold values from 0 to 63, as said below
- pair_count: int32 [32], P('sta'), may hold values from 2 to 3
Outputs:
- stacked: float32 [96, 6, 128, 128], P('sta', None, ('seg', 'band'))
Inputs may be any that keep to these rules, and one draw needn't show every extreme that they name: `pair_list`: row p belongs to index k = p // 3 of sta; its first block lies among blocks k * 2 to k * 2 + 1, which that index holds; its second block differs from the first by at most 2, on either side.
All inputs are finite; a program needn't handle non-finite values.
Results may differ from a plain program's by a relative error of at most 0.0048.
Values may be sent and summed in bfloat16 or wider, within the bound.
No kernel may reach another device: no remote copies, remote signals or barrier semaphores. Data moves between devices by JAX's collectives and lax.ppermute only.
A program may use at most 128 MiB of HBM per device.

v0:
```python
import math

import jax
import jax.numpy as jnp
from jax import lax
from jax.sharding import PartitionSpec as P

F = 8192
STA = 128
GROUP = 128
LAGS = 6
PAIR_CAP = 3


epsilon = 1e-06


def padded(cells, sides, width):
    for axis, dim in sides:
        count = lax.axis_size(axis)
        ends = count - 1
        head = lax.slice_in_dim(cells, 0, width, axis=dim)
        tail = lax.slice_in_dim(cells, cells.shape[dim] - width, cells.shape[dim], axis=dim)
        cells = jnp.concatenate(
            [
                lax.ppermute(tail, axis, [(i, (i + 1) % count) for i in range(ends)]),
                cells,
                lax.ppermute(head, axis, [((i + 1) % count, i) for i in range(ends)]),
            ],
            axis=dim,
        )
    return cells


def whiten(values):
    shape_in = values.shape
    grouped = values.astype(jnp.float32).reshape(shape_in[:-1] + (shape_in[-1] // GROUP, GROUP))
    energy = jnp.mean(grouped * grouped, axis=(-3, -1), keepdims=True)
    scaled = grouped * lax.rsqrt(energy + epsilon)
    return scaled.reshape(shape_in).astype(jnp.bfloat16)


def tables(first_bin, bin_count):
    lag_value = jnp.arange(LAGS, dtype=jnp.int32) - LAGS // 2
    bins = first_bin + jnp.arange(bin_count, dtype=jnp.int32)
    product = lag_value[:, None] * bins[None, :]
    theta = product.astype(jnp.float32) * jnp.float32(math.pi / F)
    return (jnp.cos(theta), jnp.sin(theta))


def rotate_all(left, cosine, sine_table):
    left_real = left[None, :, :, 0, :].astype(jnp.float32)
    left_imag = left[None, :, :, 1, :].astype(jnp.float32)
    cos_wide = cosine[:, None, None, :]
    sin_wide = sine_table[:, None, None, :]
    rot_real = left_real * cos_wide - left_imag * sin_wide
    rot_imag = left_real * sin_wide + left_imag * cos_wide
    both = jnp.stack([rot_real, rot_imag], axis=3).astype(jnp.bfloat16)
    return both.reshape(both.shape[0], both.shape[1], both.shape[2], -1)


def pair_term(window, first_block, left_id, right_id, cosine, sine_table):
    left = lax.dynamic_slice_in_dim(window, (left_id - first_block) * STA, STA, 1)
    right = lax.dynamic_slice_in_dim(window, (right_id - first_block) * STA, STA, 1)
    rotated = rotate_all(left, cosine, sine_table)
    right_flat = right.reshape(right.shape[0], STA, -1)
    return lax.dot_general(
        rotated, right_flat, (((1, 3), (0, 2)), ((), ())), preferred_element_type=jnp.float32
    )


def gated_term(is_live, window, first_block, left_id, right_id, cosine, sine_table):

    def compute():
        return pair_term(window, first_block, left_id, right_id, cosine, sine_table)

    def nothing():
        return jnp.zeros((LAGS, STA, STA), jnp.float32)

    return lax.cond(is_live, compute, nothing)


def body(raw_spectra, pair_list, pair_count):
    whitened = whiten(raw_spectra)
    rows_dev = whitened.shape[1]
    blk_here = rows_dev // STA
    bins_dev = whitened.shape[3]
    position = lax.axis_index("sta")
    band_index = lax.axis_index("band")
    cosine, sine_table = tables(band_index * bins_dev, bins_dev)
    norm_scale = jnp.float32(1.0 / math.sqrt(F * whitened.shape[0] * lax.axis_size("seg")))
    window = padded(whitened, (("sta", 1),), rows_dev)
    first_block = (position - 1) * blk_here
    own_terms = []
    for slot_index in range(PAIR_CAP):
        own_terms.append(
            gated_term(
                slot_index < pair_count[0],
                window,
                first_block,
                pair_list[slot_index, 0],
                pair_list[slot_index, 1],
                cosine,
                sine_table,
            )
        )
    stacked_sum = lax.psum_scatter(
        jnp.stack(own_terms), ("seg", "band"), scatter_dimension=2, tiled=True
    )
    return stacked_sum * norm_scale


def solution(mesh):
    in_specs = (P("seg", "sta", None, "band"), P("sta", None), P("sta"))
    out_specs = P("sta", None, ("seg", "band"), None)
    return jax.shard_map(body, mesh=mesh, in_specs=in_specs, out_specs=out_specs, check_vma=False)
```

profile of v0, /device:TPU:6, one launch (start us, length us, event | category | flops | bytes accessed | tf_op | source)
XLA Modules:
  0.0 245.7 jit_solution(15775311522669780321)
XLA Ops:
  6.5 0.0 reduce-scatter.2.cloned.1.call-start
  6.5 6.7 %fusion.45 = f32[256,4096]{1,0:T(8,128)S(1)} fusion(bf16[1,256,2,4096]{3,2,1,0:T(2,128)(2,1)} %param.9), kind=kLoop, calls=%fused_computation.48 | loop fusion | flops 5242880 | bytes 8388608 | tf_op jit(solution)/shard_map/reduce_sum | solution.py:38
  13.3 2.7 %copy.9 = f32[32,8,32,128]{3,2,1,0:T(8,128)} copy(f32[32,8,32,128]{3,1,2,0:T(8,128)S(1)} %bitcast.78) | data formatting | bytes 8388608
  16.0 3.3 %reduce_sum.18 = f32[256,32]{1,0:T(8,128)S(1)} reduce(f32[256,32,128]{2,1,0:T(8,128)} %bitcast.76, f32[]{:T(128)} %constant.52.clone.1), dimensions={2}, to_apply=%region_1.0 | reduce | flops 1040384 | bytes 4227076 | tf_op jit(solution)/shard_map/reduce_sum | solution.py:38
  19.4 0.0 copy-start
  19.4 1.1 mul.373
  20.5 3.8 %copy.14 = f32[32,8,32,128]{3,1,2,0:T(8,128)S(1)} copy(f32[32,8,32,128]{3,2,1,0:T(8,128)S(1)} %bitcast.77) | data formatting | bytes 8388608
  24.3 0.0 copy-done
  24.3 5.6 %fusion.46 = bf16[1,256,2,4096]{3,1,2,0:T(8,128)(2,1)} fusion(f32[256,4096]{1,0:T(8,128)S(1)} %bitcast.75, bf16[1,256,2,4096]{3,2,1,0:T(2,128)(2,1)S(1)} %copy-done), kind=kLoop, calls=%fused_computation.49 | loop fusion | flops 6291456 | bytes 12582912 | tf_op jit(solution)/shard_map/convert_element_type | solution.py:40
  29.9 11.2 %collective-permute-start.1 = (bf16[1,256,2,4096]{3,1,2,0:T(8,128)(2,1)}, bf16[1,256,2,4096]{3,1,2,0:T(8,128)(2,1)}, u32[]{:S(2)}, u32[]{:S(2)}) collective-permute-start(bf16[1,256,2,4096]{3,1,2,0:T(8,128)(2,1)} %fusion.46), channel_id=1, source_target_pairs={{16,0},{32,16},{48,32},{64,48},{80,64},{96,80},{112,96},{128,112},... | collective-permute-start | bytes 12582920 | tf_op jit(solution)/shard_map/ppermute | solution.py:28
  41.1 1.9 collective-permute-start
  43.7 0.5 fusion.47
  44.3 0.0 copy-start.1
  44.3 87.0 %collective-permute-done.1 = bf16[1,256,2,4096]{3,1,2,0:T(8,128)(2,1)} collective-permute-done((bf16[1,256,2,4096]{3,1,2,0:T(8,128)(2,1)}, bf16[1,256,2,4096]{3,1,2,0:T(8,128)(2,1)}, u32[]{:S(2)}, u32[]{:S(2)}) %collective-permute-start.1) | collective-permute-done | bytes 4194336 | tf_op jit(solution)/shard_map/ppermute | solution.py:28
  131.2 6.2 %collective-permute-done = bf16[1,256,2,4096]{3,1,2,0:T(8,128)(2,1)} collective-permute-done((bf16[1,256,2,4096]{3,1,2,0:T(8,128)(2,1)}, bf16[1,256,2,4096]{3,1,2,0:T(8,128)(2,1)}, u32[]{:S(2)}, u32[]{:S(2)}) %collective-permute-start) | collective-permute-done | bytes 4194336 | tf_op jit(solution)/shard_map/ppermute | solution.py:26
  137.5 10.4 %pad_maximum_fusion = bf16[1,768,2,4096]{3,1,2,0:T(8,128)(2,1)} fusion(bf16[1,256,2,4096]{3,1,2,0:T(8,128)(2,1)} %collective-permute-done.1, bf16[1,256,2,4096]{3,1,2,0:T(8,128)(2,1)} %fusion.46, bf16[1,256,2,4096]{3,1,2,0:T(8,128)(2,1)} %collective-permute-done), kind=kLoop, calls=%fused_computation.45 | loop fusion | flops 37748736 | bytes 25165824 | tf_op jit(solution)/shard_map/concatenate | solution.py:24
  147.9 0.0 copy-done.1
  147.9 12.8 %conditional.4 = (f32[1,6,128,128]{3,2,1,0:T(8,128)S(1)}) conditional(s32[]{:T(128)} %bitcast.28, () %tuple.31, (s32[3,2]{0,1:T(2,128)S(1)}, s32[]{:T(128)}, bf16[1,768,2,4096]{3,1,2,0:T(8,128)(2,1)}, f32[6,4096]{1,0:T(8,128)S(1)}, f32[6,4096]{1,0:T(8,128)S(1)}) %tuple.52), branch_computations={%region_4.0_spmd, %region_5.0_spmd} | conditional | flops 1643118592 | bytes 38338724 | solution.py:80
  148.2 0.6 fusion.50
  150.1 2.0 fusion.27
  152.1 3.6 %subtract_convert_fusion.1 = (bf16[6,128,1,4096]{3,1,2,0:T(8,128)(2,1)S(1)}, bf16[6,128,1,4096]{3,1,2,0:T(8,128)(2,1)S(1)}) fusion(f32[6,4096]{1,0:T(8,128)S(1)} %get-tuple-element.71, f32[128,4096]{1,0:T(8,128)S(1)} %get-tuple-element.84, f32[6,4096]{1,0:T(8,128)S(1)} %get-tuple-element.70, f32[128,4096]{1,0:T(8,128)S(1)} %get-tuple-element.83), kind=kLoop, calls=%fused_computation.20 | loop fusion | flops 25165824 | bytes 16973824 | tf_op jit(solution)/shard_map/convert.6
  155.7 5.1 %fusion.21 = f32[1,6,128,128]{3,2,1,0:T(8,128)S(1)} fusion(bf16[1,768,2,4096]{3,1,2,0:T(8,128)(2,1)} %get-tuple-element.67, s32[]{:T(128)S(6)} %select_n.15, bf16[6,128,1,4096]{3,1,2,0:T(8,128)(2,1)S(1)} %get-tuple-element.86, bf16[6,128,1,4096]{3,1,2,0:T(8,128)(2,1)S(1)} %get-tuple-element.85), kind=kOutput, calls=%fused_computation.23 | convolution fusion | flops 1616904192 | bytes 15073284 | tf_op jit(solution)/shard_map/cond/branch_1_fun/dot_general | solution.py:67
  160.8 12.5 %conditional.3 = (f32[1,6,128,128]{3,2,1,0:T(8,128)S(1)}) conditional(s32[]{:T(128)} %bitcast.27, () %tuple.29, (s32[3,2]{0,1:T(2,128)S(1)}, s32[]{:T(128)}, bf16[1,768,2,4096]{3,1,2,0:T(8,128)(2,1)}, f32[6,4096]{1,0:T(8,128)S(1)}, f32[6,4096]{1,0:T(8,128)S(1)}) %tuple.53), branch_computations={%region_2.0_spmd, %region_3.0_spmd} | conditional | flops 1643118592 | bytes 38338724 | solution.py:80
  160.8 0.5 fusion.49
  162.6 2.0 fusion.12
  164.7 3.6 %subtract_convert_fusion = (bf16[6,128,1,4096]{3,1,2,0:T(8,128)(2,1)S(1)}, bf16[6,128,1,4096]{3,1,2,0:T(8,128)(2,1)S(1)}) fusion(f32[6,4096]{1,0:T(8,128)S(1)} %get-tuple-element.66, f32[128,4096]{1,0:T(8,128)S(1)} %get-tuple-element.78, f32[6,4096]{1,0:T(8,128)S(1)} %get-tuple-element.65, f32[128,4096]{1,0:T(8,128)S(1)} %get-tuple-element.77), kind=kLoop, calls=%fused_computation.5 | loop fusion | flops 25165824 | bytes 16973824 | tf_op jit(solution)/shard_map/convert.2
  168.3 5.1 %fusion.6 = f32[1,6,128,128]{3,2,1,0:T(8,128)S(1)} fusion(bf16[1,768,2,4096]{3,1,2,0:T(8,128)(2,1)} %get-tuple-element.62, s32[]{:T(128)S(6)} %select_n.13, bf16[6,128,1,4096]{3,1,2,0:T(8,128)(2,1)S(1)} %get-tuple-element.80, bf16[6,128,1,4096]{3,1,2,0:T(8,128)(2,1)S(1)} %get-tuple-element.79), kind=kOutput, calls=%fused_computation.8 | convolution fusion | flops 1616904192 | bytes 15073284 | tf_op jit(solution)/shard_map/cond/branch_1_fun/dot_general | solution.py:67
  173.3 1.1 pad_maximum_fusion.1
  174.5 0.0 reduce-scatter.2.cloned.1.call-update
  174.5 62.9 %reduce-scatter.2.cloned.1.call-done = f32[3,6,8,128]{3,2,1,0:T(8,128)} async-done(((f32[3,6,128,128]{3,2,1,0:T(8,128)}), f32[3,6,8,128]{3,2,1,0:T(8,128)}) %reduce-scatter.2.cloned.1.call-update) | async-done | bytes 73744 | tf_op jit(solution)/shard_map/reduce_scatter | solution.py:107
  237.4 1.5 broadcast_multiply_fusion
  (5 shorter events, 0.1 us)
Async XLA Ops:
  6.5 230.8 %reduce-scatter.2.cloned.1.call-start = ((), (), s32[]{:S(2)}) async-start(), calls=%async_computation.1 | async-start | bytes 1253376 | tf_op jit(solution)/shard_map/reduce_scatter | solution.py:107
  19.4 5.0 %copy-start = (bf16[1,256,2,4096]{3,2,1,0:T(2,128)(2,1)S(1)}, bf16[1,256,2,4096]{3,2,1,0:T(2,128)(2,1)}, u32[]{:S(2)}) copy-start(bf16[1,256,2,4096]{3,2,1,0:T(2,128)(2,1)} %param.9) | copy-start | bytes 12582916
  29.9 101.3 %collective-permute-start.1 = (bf16[1,256,2,4096]{3,1,2,0:T(8,128)(2,1)}, bf16[1,256,2,4096]{3,1,2,0:T(8,128)(2,1)}, u32[]{:S(2)}, u32[]{:S(2)}) collective-permute-start(bf16[1,256,2,4096]{3,1,2,0:T(8,128)(2,1)} %fusion.46), channel_id=1, source_target_pairs={{16,0},{32,16},{48,32},{64,48},{80,64},{96,80},{112,96},{128,112},... | collective-permute-start | bytes 12582920 | tf_op jit(solution)/shard_map/ppermute | solution.py:28
  41.1 96.4 %collective-permute-start = (bf16[1,256,2,4096]{3,1,2,0:T(8,128)(2,1)}, bf16[1,256,2,4096]{3,1,2,0:T(8,128)(2,1)}, u32[]{:S(2)}, u32[]{:S(2)}) collective-permute-start(bf16[1,256,2,4096]{3,1,2,0:T(8,128)(2,1)} %fusion.46), channel_id=1, source_target_pairs={{0,16},{16,32},{32,48},{48,64},{64,80},{80,96},{96,112},{112,128},... | collective-permute-start | bytes 12582920 | tf_op jit(solution)/shard_map/ppermute | solution.py:26
  44.3 103.6 %copy-start.1 = (s32[3,2]{0,1:T(2,128)S(1)}, s32[3,2]{0,1:T(2,128)}, u32[]{:S(2)}) copy-start(s32[3,2]{0,1:T(2,128)} %param.10) | copy-start | bytes 76
Sparse Core Ops, SparseCore 0:
  174.6 62.7 reduce-scatter.1
where the time goes:
time: 246 us
  waiting for transfers between devices  156 us (63%)
  other arithmetic  40.5 us (16%)
  between operations  14.2 us (6%)
  starting transfers between devices  13.1 us (5%)
  matrix products  10.2 us (4%)
  local copies, waits for them, and re-layouts  8.84 us (4%)
  loops' own time  2.84 us (1%)
    ppermute x1, waiting for transfers between devices, padded(): lax.ppermute(head, axis, [((i + 1) % count, i) for i in range(ends)])  87 us
    reduce_scatter x1, waiting for transfers between devices, body(): lax.psum_scatter(jnp.stack(own_terms), ('seg', 'band'), scatter_dimension...  62.9 us
    ppermute x1, starting transfers between devices, padded(): lax.ppermute(head, axis, [((i + 1) % count, i) for i in range(ends)])  11.2 us
    concatenate x1, other arithmetic, padded(): jnp.concatenate([lax.ppermute(tail, axis, [(i, (i + 1) % count) for i in...  10.4 us
    dot_general x2, matrix products, pair_term(): lax.dot_general(rotated, right_flat, (((1, 3), (0, 2)), ((), ())), prefer...  10.2 us
    reduce_sum x2, other arithmetic, whiten(): energy = jnp.mean(grouped * grouped, axis=(-3, -1), keepdims=True)  10.1 us
    another operation x2, other arithmetic  7.17 us
    unnamed x6, local copies, waits for them, and re-layouts  6.51 us
  transfers between devices with their start and end apart: 3, of which 3 were waited for; matrix products, arithmetic and copies ran while one was open for 0% of the time, Pallas kernels for 0%

commit v1 on v0

v1 whole, which is shorter than its diff:
```python
import functools
import math

import jax
import jax.numpy as jnp
from jax import lax
from jax.experimental import pallas as pl
from jax.experimental.pallas import tpu as pltpu
from jax.sharding import PartitionSpec as P

F = 8192
STA = 128
GROUP = 128
LAGS = 6
PAIR_CAP = 3
TURNS = 3
STEP = 512
EPSILON = 1e-06
FROM_LEFT, FROM_RIGHT, LOCAL, REMOTE, DEAD = 0, 1, 2, 3, 4
CHUNKS = (3072, 1024)


def tables(first_bin, bin_count):
    turn = 1 + jnp.arange(TURNS, dtype=jnp.int32)
    bins = first_bin + jnp.arange(bin_count, dtype=jnp.int32)
    theta = (turn[:, None] * bins[None, :]).astype(jnp.float32) * jnp.float32(math.pi / F)
    return jnp.concatenate([jnp.cos(theta), jnp.sin(theta), jnp.zeros((2, bin_count), jnp.float32)])


def whiten(values):
    real, imag = values[0].astype(jnp.float32), values[1].astype(jnp.float32)
    power = real * real + imag * imag
    parts = []
    for start in range(0, power.shape[1], GROUP):
        energy = jnp.sum(power[:, start : start + GROUP], axis=1, keepdims=True) * (1.0 / (2 * GROUP))
        scale = lax.rsqrt(energy + EPSILON)
        parts.append(
            (
                (real[:, start : start + GROUP] * scale).astype(jnp.bfloat16),
                (imag[:, start : start + GROUP] * scale).astype(jnp.bfloat16),
            )
        )
    return jnp.concatenate([p[0] for p in parts], axis=1), jnp.concatenate([p[1] for p in parts], axis=1)


def put_rotations(turned, block, real16, imag16, table, top):
    width = real16.shape[1]
    count = TURNS + 1 + top
    base = block * count * STA
    real, imag = real16.astype(jnp.float32), imag16.astype(jnp.float32)

    def put(turn, re, im):
        at = base + (turn + TURNS) * STA
        turned[at : at + STA, :width] = re
        turned[at : at + STA, width:] = im

    put(0, real16, imag16)
    for turn in range(1, TURNS + 1):
        cos, sin = table[turn - 1 : turn, :], table[TURNS + turn - 1 : TURNS + turn, :]
        real_cos, imag_sin = real * cos, imag * sin
        real_sin, imag_cos = real * sin, imag * cos
        if turn <= top:
            put(turn, (real_cos - imag_sin).astype(jnp.bfloat16), (real_sin + imag_cos).astype(jnp.bfloat16))
        put(-turn, (real_cos + imag_sin).astype(jnp.bfloat16), (imag_cos - real_sin).astype(jnp.bfloat16))


def product(rows, columns):
    return lax.dot_general(rows, columns, (((1,), (1,)), ((), ())), preferred_element_type=jnp.float32)


def local_kernel(info, first, second, table_ref, white_ref, local_ref, turned, sums):
    step = pl.program_id(0)

    @pl.when(step == 0)
    def _():
        sums[...] = jnp.zeros_like(sums)

    table = table_ref[...]
    for block, source in enumerate((first, second)):
        real16, imag16 = whiten(source)
        white_ref[block * STA : (block + 1) * STA, :STEP] = real16
        white_ref[block * STA : (block + 1) * STA, STEP:] = imag16
        put_rotations(turned, block, real16, imag16, table, TURNS - 1)
    sums[...] += product(turned[...], white_ref[...])

    @pl.when(step == pl.num_programs(0) - 1)
    def _():
        for slot in range(PAIR_CAP):
            here = info[slot] == LOCAL

            @pl.when(here)
            def _():
                row = pl.multiple_of(info[3 + slot] * (LAGS * STA), LAGS * STA)
                column = pl.multiple_of(info[6 + slot] * STA, STA)
                local_ref[slot] = sums[pl.ds(row, LAGS * STA), pl.ds(column, STA)]

            @pl.when(jnp.logical_not(here))
            def _():
                local_ref[slot] = jnp.zeros((LAGS * STA, STA), jnp.float32)


def local_part(info, first, second, table):
    bins = table.shape[1]
    steps = bins // STEP
    block = pl.BlockSpec((2, STA, STEP), lambda i, info: (0, 0, i))
    return pl.pallas_call(
        local_kernel,
        out_shape=(
            jax.ShapeDtypeStruct((2 * STA, 2 * bins), jnp.bfloat16),
            jax.ShapeDtypeStruct((PAIR_CAP, LAGS * STA, STA), jnp.float32),
        ),
        grid_spec=pltpu.PrefetchScalarGridSpec(
            num_scalar_prefetch=1,
            grid=(steps,),
            in_specs=[block, block, pl.BlockSpec((8, STEP), lambda i, info: (0, i))],
            out_specs=(
                pl.BlockSpec((2 * STA, 2 * STEP), lambda i, info: (0, i)),
                pl.BlockSpec((PAIR_CAP, LAGS * STA, STA), lambda i, info: (0, 0, 0)),
            ),
            scratch_shapes=[
                pltpu.VMEM((2 * LAGS * STA, 2 * STEP), jnp.bfloat16),
                pltpu.VMEM((2 * LAGS * STA, 2 * STA), jnp.float32),
            ],
        ),
        compiler_params=pltpu.CompilerParams(vmem_limit_bytes=32 << 20),
        cost_estimate=pl.CostEstimate(flops=2 * 2 * LAGS * STA * 2 * STA * 2 * bins, bytes_accessed=16 << 20, transcendentals=0),
        name="local_pairs",
    )(info, first, second, table)


ALL_TURNS = 2 * TURNS + 1
SUM_ROWS = 2 * ALL_TURNS * STA
OUT_ROWS = (PAIR_CAP + 2) * LAGS * 8


def accumulate(step, left, right, table_ref, white_ref, turned, sums):
    table = table_ref[...]
    for block, source in enumerate((left, right)):
        real16, imag16 = whiten(source)
        put_rotations(turned, block, real16, imag16, table, TURNS)
    sums[...] += product(turned[...], white_ref[...])


def remote_kernel(left, right, table_ref, white_ref, sums_ref, turned):
    step = pl.program_id(0)

    @pl.when(step == 0)
    def _():
        sums_ref[...] = jnp.zeros_like(sums_ref)

    accumulate(step, left, right, table_ref, white_ref, turned, sums_ref)


def last_kernel(info, left, right, table_ref, white_ref, before, local_ref, keep_ref, send_ref, turned, sums, stage):
    step = pl.program_id(0)

    @pl.when(step == 0)
    def _():
        sums[...] = before[...]

    accumulate(step, left, right, table_ref, white_ref, turned, sums)

    @pl.when(step == pl.num_programs(0) - 1)
    def _():
        def put(place, tile):
            octets = tile.reshape(8, 2, 8, STA)
            for core in range(2):
                stage[core, :, place * 8 : place * 8 + 8, :] = octets[:, core]

        for slot in range(PAIR_CAP):
            kind = info[slot]

            @pl.when(kind < LOCAL)
            def _():
                column = pl.multiple_of(info[3 + slot] * STA, STA)
                for lag in range(LAGS):
                    row = pl.multiple_of((kind * ALL_TURNS + 2 * TURNS - lag) * STA, STA)
                    put(slot * LAGS + lag, sums[pl.ds(row, STA), pl.ds(column, STA)].T)

            @pl.when(kind >= LOCAL)
            def _():
                for lag in range(LAGS):
                    put(slot * LAGS + lag, local_ref[slot, lag * STA : (lag + 1) * STA, :])

        for lag in range(LAGS):
            row = (ALL_TURNS + lag) * STA
            put(PAIR_CAP * LAGS + lag, sums[row : row + STA, :STA])
            row = lag * STA
            put((PAIR_CAP + 1) * LAGS + lag, sums[row : row + STA, STA:])
        core = info[9]
        keep_ref[...] = stage[core]
        send_ref[...] = stage[1 - core].astype(jnp.bfloat16)


def remote_specs(base, prefetch):
    block = pl.BlockSpec((2, STA, STEP), lambda i, *_: (0, 0, i))
    return [
        block,
        block,
        pl.BlockSpec((8, STEP), lambda i, *_: (0, base + i)),
        pl.BlockSpec((2 * STA, 2 * STEP), lambda i, *_: (0, base + i)),
    ]


def remote_cost(bins):
    return pl.CostEstimate(flops=2 * SUM_ROWS * 2 * STA * 2 * bins, bytes_accessed=8 << 20, transcendentals=0)


def remote_part(left, right, table, white, first_bin):
    bins = left.shape[2]
    return pl.pallas_call(
        remote_kernel,
        out_shape=jax.ShapeDtypeStruct((SUM_ROWS, 2 * STA), jnp.float32),
        grid=(bins // STEP,),
        in_specs=remote_specs(first_bin // STEP, False),
        out_specs=pl.BlockSpec((SUM_ROWS, 2 * STA), lambda i: (0, 0)),
        scratch_shapes=[pltpu.VMEM((SUM_ROWS, 2 * STEP), jnp.bfloat16)],
        compiler_params=pltpu.CompilerParams(vmem_limit_bytes=32 << 20),
        cost_estimate=remote_cost(bins),
        name="remote_pairs",
    )(left, right, table, white)


def last_part(info, left, right, table, white, before, local, first_bin):
    bins = left.shape[2]
    whole = lambda shape: pl.BlockSpec(shape, lambda i, *_: (0,) * len(shape))
    return pl.pallas_call(
        last_kernel,
        out_shape=(
            jax.ShapeDtypeStruct((8, OUT_ROWS, STA), jnp.float32),
            jax.ShapeDtypeStruct((8, OUT_ROWS, STA), jnp.bfloat16),
        ),
        grid_spec=pltpu.PrefetchScalarGridSpec(
            num_scalar_prefetch=1,
            grid=(bins // STEP,),
            in_specs=remote_specs(first_bin // STEP, True) + [whole((SUM_ROWS, 2 * STA)), whole(local.shape)],
            out_specs=(whole((8, OUT_ROWS, STA)), whole((8, OUT_ROWS, STA))),
            scratch_shapes=[
                pltpu.VMEM((SUM_ROWS, 2 * STEP), jnp.bfloat16),
                pltpu.VMEM((SUM_ROWS, 2 * STA), jnp.float32),
                pltpu.VMEM((2, 8, OUT_ROWS, STA), jnp.float32),
            ],
        ),
        compiler_params=pltpu.CompilerParams(vmem_limit_bytes=40 << 20),
        cost_estimate=remote_cost(bins),
        name="last_pairs",
    )(info, left, right, table, white, before, local)


def body(raw_spectra, pair_list, pair_count):
    bins_dev = raw_spectra.shape[3]
    sta_count = lax.axis_size("sta")
    position = lax.axis_index("sta")
    core = lax.axis_index("band")
    to_right = [(i, i + 1) for i in range(sta_count - 1)]
    to_left = [(i + 1, i) for i in range(sta_count - 1)]

    planes = []
    received = []
    start = 0
    for count in CHUNKS:
        cut = raw_spectra[0, :, :, start : start + count]
        first = jnp.transpose(cut[:STA], (1, 0, 2))
        second = jnp.transpose(cut[STA:], (1, 0, 2))
        planes.append((first, second))
        received.append((lax.ppermute(second, "sta", to_right), lax.ppermute(first, "sta", to_left)))
        start += count

    own = pair_list - position * 2
    left_id, right_id = own[:, 0], own[:, 1]
    kind = jnp.where(right_id == -1, FROM_LEFT, jnp.where(right_id == 2, FROM_RIGHT, LOCAL))
    kind = jnp.where((right_id == -2) | (right_id == 3), REMOTE, kind)
    kind = jnp.where(jnp.arange(PAIR_CAP) < pair_count[0], kind, DEAD)
    info = jnp.concatenate([kind, left_id, right_id, core[None]]).astype(jnp.int32)
    table = tables(core * bins_dev, bins_dev)

    first = jnp.concatenate([p[0] for p in planes], axis=2)
    second = jnp.concatenate([p[1] for p in planes], axis=2)
    white, local = local_part(info, first, second, table)
    before = remote_part(*received[0], table, white, 0)
    keep, send = last_part(info, *received[1], table, white, before, local, CHUNKS[0])

    other = lax.ppermute(send, "band", [(0, 1), (1, 0)])
    pieces = (keep + other.astype(jnp.float32)).astype(jnp.bfloat16)
    gathered = lax.all_to_all(pieces, "seg", 0, 0)
    scale = jnp.float32(1.0 / math.sqrt(F * raw_spectra.shape[0] * lax.axis_size("seg")))
    totals = jnp.sum(gathered.astype(jnp.float32), axis=0) * scale
    totals = totals.reshape(PAIR_CAP + 2, LAGS, 8, STA)
    from_left = lax.ppermute(totals[PAIR_CAP], "sta", to_right)
    from_right = lax.ppermute(totals[PAIR_CAP + 1], "sta", to_left)
    remote = (kind == REMOTE)[:, None, None, None]
    is_left = (right_id < 0)[:, None, None, None]
    return jnp.where(remote, jnp.where(is_left, from_left[None], from_right[None]), totals[:PAIR_CAP])


def solution(mesh):
    in_specs = (P("seg", "sta", None, "band"), P("sta", None), P("sta"))
    out_specs = P("sta", None, ("seg", "band"), None)
    return jax.shard_map(body, mesh=mesh, in_specs=in_specs, out_specs=out_specs, check_vma=False)
```

time: 246 us -> 119 us (0.48)
  waiting for transfers between devices: 156 us -> 21.3 us
  other arithmetic: 40.5 us -> 6.47 us
  Pallas kernels: 0 us -> 25.8 us
  blocking collectives: 0 us -> 24 us
  starting transfers between devices: 13.1 us -> 28.8 us
  between operations: 14.2 us -> 0.9 us
  matrix products: 10.2 us -> 0 us
  local copies, waits for them, and re-layouts: 8.84 us -> 11.8 us
  loops' own time: 2.84 us -> 0 us
    ppermute x2 -> x7, waiting for transfers between devices: 93.2 us -> 21.3 us  [the longest x2 13.5 us: body(): lax.ppermute(first, 'sta', to_left)]
    reduce_scatter x1 -> x0, waiting for transfers between devices: 62.9 us -> none  [body(): lax.psum_scatter(jnp.stack(own_terms), ('seg', 'band'), scatter_dimension...]
    pallas_call x0 -> x3, Pallas kernels: none -> 25.8 us  [the longest x1 11.7 us: local_part(): pl.pallas_call(local_kernel, out_shape=(jax.ShapeDtypeStruct((2 * STA, 2...]
    all_to_all x0 -> x1, blocking collectives: none -> 24 us  [body(): gathered = lax.all_to_all(pieces, 'seg', 0, 0)]
    ppermute x2 -> x7, starting transfers between devices: 13.1 us -> 28.8 us  [the longest x2 12.8 us: body(): lax.ppermute(first, 'sta', to_left)]
    dot_general x2 -> x0, matrix products: 10.2 us -> none  [pair_term(): lax.dot_general(rotated, right_flat, (((1, 3), (0, 2)), ((), ())), prefer...]
    reduce_sum x2 -> x1, other arithmetic: 10.1 us -> 0.07 us  [body(): totals = jnp.sum(gathered.astype(jnp.float32), axis=0) * scale]
    convert_element_type x3 -> x1, other arithmetic: 9.62 us -> 0.12 us  [body(): pieces = (keep + other.astype(jnp.float32)).astype(jnp.bfloat16)]
  transfers between devices with their start and end apart: 3 -> 7, of which waited for: 3 -> 4; matrix products, arithmetic and copies ran while one was open for 0% -> 11% of each run, Pallas kernels for 0% -> 18%
where the time goes in v1:
time: 119 us
  starting transfers between devices  28.8 us (24%)
  Pallas kernels  25.8 us (22%)
  blocking collectives  24 us (20%)
  waiting for transfers between devices  21.3 us (18%)
  local copies, waits for them, and re-layouts  11.8 us (10%)
  other arithmetic  6.47 us (5%)
    all_to_all x1, blocking collectives, body(): gathered = lax.all_to_all(pieces, 'seg', 0, 0)  24 us
    ppermute x2, waiting for transfers between devices, body(): lax.ppermute(first, 'sta', to_left)  13.5 us
    ppermute x2, starting transfers between devices, body(): lax.ppermute(first, 'sta', to_left)  12.8 us
    pallas_call x1, Pallas kernels, local_part(): pl.pallas_call(local_kernel, out_shape=(jax.ShapeDtypeStruct((2 * STA, 2...  11.7 us
    pallas_call x1, Pallas kernels, remote_part(): pl.pallas_call(remote_kernel, out_shape=jax.ShapeDtypeStruct((SUM_ROWS, 2...  9.93 us
    unnamed x10, local copies, waits for them, and re-layouts  6.52 us
    ppermute x2, starting transfers between devices, body(): lax.ppermute(second, 'sta', to_right)  6.18 us
    ppermute x1, starting transfers between devices, body(): from_right = lax.ppermute(totals[PAIR_CAP + 1], 'sta', to_left)  6.03 us
  transfers between devices with their start and end apart: 7, of which 4 were waited for; matrix products, arithmetic and copies ran while one was open for 11% of the time, Pallas kernels for 18%

profile of v1, /device:TPU:6, one launch (start us, length us, event | category | flops | bytes accessed | tf_op | source)
XLA Modules:
  0.0 119.1 jit_solution(10221973609031778639)
XLA Ops:
  0.0 2.1 %fusion.3 = (bf16[1,128,2,1024]{3,2,1,0:T(2,128)(2,1)S(1)}, bf16[1,128,2,1024]{3,2,1,0:T(2,128)(2,1)S(1)}) fusion(bf16[1,256,2,4096]{3,2,1,0:T(2,128)(2,1)} %param.3), kind=kLoop, calls=%fused_computation.29 | loop fusion | bytes 2097152 | tf_op jit(solution)/shard_map/slice | solution.py:263
  2.1 1.0 copy.19
  3.0 4.3 %collective-permute-start = (bf16[2,128,1024]{2,1,0:T(8,128)(2,1)}, bf16[2,128,1024]{2,1,0:T(8,128)(2,1)S(1)}, u32[]{:S(2)}, u32[]{:S(2)}) collective-permute-start(bf16[2,128,1024]{2,1,0:T(8,128)(2,1)} %bitcast.35), channel_id=1, source_target_pairs={{0,16},{16,32},{32,48},{48,64},{64,80},{80,96},{96,112},{112,128},... | collective-permute-start | bytes 1572872 | tf_op jit(solution)/shard_map/ppermute | solution.py:266
  7.3 0.9 copy.18
  8.3 8.8 %collective-permute-start.1 = (bf16[2,128,1024]{2,1,0:T(8,128)(2,1)}, bf16[2,128,1024]{2,1,0:T(8,128)(2,1)S(1)}, u32[]{:S(2)}, u32[]{:S(2)}) collective-permute-start(bf16[2,128,1024]{2,1,0:T(8,128)(2,1)} %bitcast.34), channel_id=1, source_target_pairs={{16,0},{32,16},{48,32},{64,48},{80,64},{96,80},{112,96},{128,112},... | collective-permute-start | bytes 1572872 | tf_op jit(solution)/shard_map/ppermute | solution.py:266
  17.1 3.1 %fusion.2 = (bf16[1,128,2,3072]{3,2,1,0:T(2,128)(2,1)S(1)}, bf16[1,128,2,3072]{3,2,1,0:T(2,128)(2,1)S(1)}) fusion(bf16[1,256,2,4096]{3,2,1,0:T(2,128)(2,1)S(1)} %copy-done.1), kind=kLoop, calls=%fused_computation.28 | loop fusion | bytes 6291456 | tf_op jit(solution)/shard_map/slice | solution.py:264
  20.2 1.5 %copy.17 = bf16[1,128,2,3072]{3,1,2,0:T(8,128)(2,1)} copy(bf16[1,128,2,3072]{3,2,1,0:T(2,128)(2,1)S(1)} %get-tuple-element.16) | data formatting | bytes 3145728
  21.7 3.9 %collective-permute-start.3 = (bf16[2,128,3072]{2,1,0:T(8,128)(2,1)}, bf16[2,128,3072]{2,1,0:T(8,128)(2,1)}, u32[]{:S(2)}, u32[]{:S(2)}) collective-permute-start(bf16[2,128,3072]{2,1,0:T(8,128)(2,1)} %bitcast.33), channel_id=1, source_target_pairs={{16,0},{32,16},{48,32},{64,48},{80,64},{96,80},{112,96},{128,112},... | collective-permute-start | bytes 4718600 | tf_op jit(solution)/shard_map/ppermute | solution.py:266
  25.7 1.5 %copy.16 = bf16[1,128,2,3072]{3,1,2,0:T(8,128)(2,1)} copy(bf16[1,128,2,3072]{3,2,1,0:T(2,128)(2,1)S(1)} %get-tuple-element.15) | data formatting | bytes 3145728
  27.2 1.9 %collective-permute-start.2 = (bf16[2,128,3072]{2,1,0:T(8,128)(2,1)}, bf16[2,128,3072]{2,1,0:T(8,128)(2,1)}, u32[]{:S(2)}, u32[]{:S(2)}) collective-permute-start(bf16[2,128,3072]{2,1,0:T(8,128)(2,1)} %bitcast.32), channel_id=1, source_target_pairs={{0,16},{16,32},{32,48},{48,64},{64,80},{80,96},{96,112},{112,128},... | collective-permute-start | bytes 4718600 | tf_op jit(solution)/shard_map/ppermute | solution.py:266
  29.1 1.7 %pad_maximum_fusion.1.second = bf16[2,128,4096]{2,1,0:T(8,128)(2,1)S(1)} fusion(bf16[2,128,1024]{2,1,0:T(8,128)(2,1)} %bitcast.35, bf16[2,128,3072]{2,1,0:T(8,128)(2,1)} %bitcast.32), kind=kLoop, calls=%fused_computation.1 | loop fusion | flops 4194304 | bytes 4194304 | tf_op jit(solution)/shard_map/concatenate | solution.py:278
  30.9 0.0 copy-start.2
  30.9 3.1 %pad_maximum_fusion.first = bf16[2,128,4096]{2,1,0:T(8,128)(2,1)} fusion(bf16[2,128,1024]{2,1,0:T(8,128)(2,1)} %bitcast.34, bf16[2,128,3072]{2,1,0:T(8,128)(2,1)} %bitcast.33), kind=kLoop, calls=%fused_computation | loop fusion | flops 4194304 | bytes 4194304 | tf_op jit(solution)/shard_map/concatenate | solution.py:277
  34.7 0.1 pad.6.clone
  34.8 0.5 fusion.1
  35.3 0.1 pad_add_fusion.info
  35.4 0.1 maximum_maximum_fusion.table_ref
  35.5 1.6 %copy-done = bf16[2,128,4096]{2,1,0:T(8,128)(2,1)S(1)} copy-done((bf16[2,128,4096]{2,1,0:T(8,128)(2,1)S(1)}, bf16[2,128,4096]{2,1,0:T(8,128)(2,1)}, u32[]{:S(2)}) %copy-start) | copy-done | bytes 2097176
  37.1 11.7 %local_pairs.1 = (bf16[256,8192]{1,0:T(8,128)(2,1)S(1)}, f32[3,768,128]{2,1,0:T(8,128)S(1)}) custom-call(s32[10]{0:T(128)S(1)} %pad_add_fusion.info, bf16[2,128,4096]{2,1,0:T(8,128)(2,1)S(1)} %copy-done, bf16[2,128,4096]{2,1,0:T(8,128)(2,1)S(1)} %pad_maximum_fusion.1.second, f32[8,4096]{1,0:T(8,128)S(1)} %maximum_maximum_fusion.table_ref), custom_call_target="tpu_custom_call" | custom-call | flops 6442450944 | bytes 16777216 | tf_op jit(solution)/shard_map/local_pairs/pallas_call | solution.py:106
  48.8 13.5 %collective-permute-done.3.right = bf16[2,128,3072]{2,1,0:T(8,128)(2,1)} collective-permute-done((bf16[2,128,3072]{2,1,0:T(8,128)(2,1)}, bf16[2,128,3072]{2,1,0:T(8,128)(2,1)}, u32[]{:S(2)}, u32[]{:S(2)}) %collective-permute-start.3) | collective-permute-done | bytes 1572896 | tf_op jit(solution)/shard_map/ppermute | solution.py:266
  62.3 4.5 %collective-permute-done.2.left = bf16[2,128,3072]{2,1,0:T(8,128)(2,1)} collective-permute-done((bf16[2,128,3072]{2,1,0:T(8,128)(2,1)}, bf16[2,128,3072]{2,1,0:T(8,128)(2,1)}, u32[]{:S(2)}, u32[]{:S(2)}) %collective-permute-start.2) | collective-permute-done | bytes 1572896 | tf_op jit(solution)/shard_map/ppermute | solution.py:266
  66.8 9.9 %remote_pairs.1.before = f32[1792,256]{1,0:T(8,128)S(1)} custom-call(bf16[2,128,3072]{2,1,0:T(8,128)(2,1)} %collective-permute-done.2.left, bf16[2,128,3072]{2,1,0:T(8,128)(2,1)} %collective-permute-done.3.right, f32[8,4096]{1,0:T(8,128)S(1)} %maximum_maximum_fusion.table_ref, bf16[256,8192]{1,0:T(8,128)(2,1)S(1)} %get-tuple-element.9.white_ref), custom_call_target="tpu_custom_call" | custom-call | flops 5637144576 | bytes 8388608 | tf_op jit(solution)/shard_map/remote_pairs/pallas_call | solution.py:211
  76.7 4.2 %last_pairs.1 = (f32[8,240,128]{2,1,0:T(8,128)S(1)}, bf16[8,240,128]{2,1,0:T(8,128)(2,1)S(1)}) custom-call(s32[10]{0:T(128)S(1)} %pad_add_fusion.info, bf16[2,128,1024]{2,1,0:T(8,128)(2,1)S(1)} %collective-permute-done.left, bf16[2,128,1024]{2,1,0:T(8,128)(2,1)S(1)} %collective-permute-done.1.right, f32[8,4096]{1,0:T(8,128)S(1)} %maximum_maximum_fusion.table_ref, ...), custom_call_target="tpu_custom_call" | custom-call | flops 1879048192 | bytes 8388608 | tf_op jit(solution)/shard_map/last_pairs/pallas_call | solution.py:227
  80.9 1.9 %collective-permute-start.4 = (bf16[8,240,128]{2,1,0:T(8,128)(2,1)S(1)}, bf16[8,240,128]{2,1,0:T(8,128)(2,1)S(1)}, u32[]{:S(2)}, u32[]{:S(2)}) collective-permute-start(bf16[8,240,128]{2,1,0:T(8,128)(2,1)S(1)} %get-tuple-element.12), channel_id=1, source_target_pairs={{0,1},{1,0},{2,3},{3,2},{4,5},{5,4},{6,7},{7,6},{8,9},{9,8},{10,11... | collective-permute-start | bytes 1474568 | tf_op jit(solution)/shard_map/ppermute | solution.py:283
  82.9 1.8 %collective-permute-done.4 = bf16[8,240,128]{2,1,0:T(8,128)(2,1)S(1)} collective-permute-done((bf16[8,240,128]{2,1,0:T(8,128)(2,1)S(1)}, bf16[8,240,128]{2,1,0:T(8,128)(2,1)S(1)}, u32[]{:S(2)}, u32[]{:S(2)}) %collective-permute-start.4) | collective-permute-done | bytes 491552 | tf_op jit(solution)/shard_map/ppermute | solution.py:283
  84.7 0.1 add_convert_fusion
  84.8 24.0 %all_to_all.5 = bf16[8,240,128]{2,1,0:T(8,128)(2,1)S(1)} all-to-all(bf16[8,240,128]{2,1,0:T(8,128)(2,1)S(1)} %add_convert_fusion), channel_id=1, replica_groups=mesh['sta'=32,'seg'=8,'band'=2] {'seg'}, dimensions={0} | all-to-all | bytes 983040 | tf_op jit(solution)/shard_map/all_to_all | solution.py:285
  108.8 0.1 convert_reduce_fusion
  108.9 1.9 %collective-permute-start.5 = (f32[6,8,128]{2,1,0:T(8,128)S(1)}, f32[6,8,128]{2,1,0:T(8,128)S(1)}, u32[]{:S(2)}, u32[]{:S(2)}) collective-permute-start(f32[6,8,128]{2,1,0:T(8,128)S(1)} %get-tuple-element.19), channel_id=1, source_target_pairs={{0,16},{16,32},{32,48},{48,64},{64,80},{80,96},{96,112},{112,128},... | collective-permute-start | bytes 73736 | tf_op jit(solution)/shard_map/ppermute | solution.py:289
  110.8 6.0 %collective-permute-start.6 = (f32[6,8,128]{2,1,0:T(8,128)S(1)}, f32[6,8,128]{2,1,0:T(8,128)S(1)}, u32[]{:S(2)}, u32[]{:S(2)}) collective-permute-start(f32[6,8,128]{2,1,0:T(8,128)S(1)} %get-tuple-element.20), channel_id=1, source_target_pairs={{16,0},{32,16},{48,32},{64,48},{80,64},{96,80},{112,96},{128,112},... | collective-permute-start | bytes 73736 | tf_op jit(solution)/shard_map/ppermute | solution.py:290
  116.9 1.5 %collective-permute-done.6 = f32[6,8,128]{2,1,0:T(8,128)S(1)} collective-permute-done((f32[6,8,128]{2,1,0:T(8,128)S(1)}, f32[6,8,128]{2,1,0:T(8,128)S(1)}, u32[]{:S(2)}, u32[]{:S(2)}) %collective-permute-start.6) | collective-permute-done | bytes 24608 | tf_op jit(solution)/shard_map/ppermute | solution.py:290
  118.4 0.7 select_select_fusion
  (16 shorter events, 0.1 us)
Async XLA Ops:
  0.0 17.1 %copy-start.1 = (bf16[1,256,2,4096]{3,2,1,0:T(2,128)(2,1)S(1)}, bf16[1,256,2,4096]{3,2,1,0:T(2,128)(2,1)}, u32[]{:S(2)}) copy-start(bf16[1,256,2,4096]{3,2,1,0:T(2,128)(2,1)} %param.3) | copy-start | bytes 12582916
  3.0 73.7 %collective-permute-start = (bf16[2,128,1024]{2,1,0:T(8,128)(2,1)}, bf16[2,128,1024]{2,1,0:T(8,128)(2,1)S(1)}, u32[]{:S(2)}, u32[]{:S(2)}) collective-permute-start(bf16[2,128,1024]{2,1,0:T(8,128)(2,1)} %bitcast.35), channel_id=1, source_target_pairs={{0,16},{16,32},{32,48},{48,64},{64,80},{80,96},{96,112},{112,128},... | collective-permute-start | bytes 1572872 | tf_op jit(solution)/shard_map/ppermute | solution.py:266
  8.3 68.5 %collective-permute-start.1 = (bf16[2,128,1024]{2,1,0:T(8,128)(2,1)}, bf16[2,128,1024]{2,1,0:T(8,128)(2,1)S(1)}, u32[]{:S(2)}, u32[]{:S(2)}) collective-permute-start(bf16[2,128,1024]{2,1,0:T(8,128)(2,1)} %bitcast.34), channel_id=1, source_target_pairs={{16,0},{32,16},{48,32},{64,48},{80,64},{96,80},{112,96},{128,112},... | collective-permute-start | bytes 1572872 | tf_op jit(solution)/shard_map/ppermute | solution.py:266
  21.7 40.5 %collective-permute-start.3 = (bf16[2,128,3072]{2,1,0:T(8,128)(2,1)}, bf16[2,128,3072]{2,1,0:T(8,128)(2,1)}, u32[]{:S(2)}, u32[]{:S(2)}) collective-permute-start(bf16[2,128,3072]{2,1,0:T(8,128)(2,1)} %bitcast.33), channel_id=1, source_target_pairs={{16,0},{32,16},{48,32},{64,48},{80,64},{96,80},{112,96},{128,112},... | collective-permute-start | bytes 4718600 | tf_op jit(solution)/shard_map/ppermute | solution.py:266
  27.2 39.6 %collective-permute-start.2 = (bf16[2,128,3072]{2,1,0:T(8,128)(2,1)}, bf16[2,128,3072]{2,1,0:T(8,128)(2,1)}, u32[]{:S(2)}, u32[]{:S(2)}) collective-permute-start(bf16[2,128,3072]{2,1,0:T(8,128)(2,1)} %bitcast.32), channel_id=1, source_target_pairs={{0,16},{16,32},{32,48},{48,64},{64,80},{80,96},{96,112},{112,128},... | collective-permute-start | bytes 4718600 | tf_op jit(solution)/shard_map/ppermute | solution.py:266
  30.9 3.8 %copy-start.2 = (s32[3,2]{0,1:T(2,128)S(1)}, s32[3,2]{0,1:T(2,128)}, u32[]{:S(2)}) copy-start(s32[3,2]{0,1:T(2,128)} %param.4) | copy-start | bytes 76
  35.5 1.6 %copy-start = (bf16[2,128,4096]{2,1,0:T(8,128)(2,1)S(1)}, bf16[2,128,4096]{2,1,0:T(8,128)(2,1)}, u32[]{:S(2)}) copy-start(bf16[2,128,4096]{2,1,0:T(8,128)(2,1)} %pad_maximum_fusion.first) | copy-start | bytes 6291460
  80.9 3.8 %collective-permute-start.4 = (bf16[8,240,128]{2,1,0:T(8,128)(2,1)S(1)}, bf16[8,240,128]{2,1,0:T(8,128)(2,1)S(1)}, u32[]{:S(2)}, u32[]{:S(2)}) collective-permute-start(bf16[8,240,128]{2,1,0:T(8,128)(2,1)S(1)} %get-tuple-element.12), channel_id=1, source_target_pairs={{0,1},{1,0},{2,3},{3,2},{4,5},{5,4},{6,7},{7,6},{8,9},{9,8},{10,11... | collective-permute-start | bytes 1474568 | tf_op jit(solution)/shard_map/ppermute | solution.py:283
  108.9 8.0 %collective-permute-start.5 = (f32[6,8,128]{2,1,0:T(8,128)S(1)}, f32[6,8,128]{2,1,0:T(8,128)S(1)}, u32[]{:S(2)}, u32[]{:S(2)}) collective-permute-start(f32[6,8,128]{2,1,0:T(8,128)S(1)} %get-tuple-element.19), channel_id=1, source_target_pairs={{0,16},{16,32},{32,48},{48,64},{64,80},{80,96},{96,112},{112,128},... | collective-permute-start | bytes 73736 | tf_op jit(solution)/shard_map/ppermute | solution.py:289
  110.8 7.5 %collective-permute-start.6 = (f32[6,8,128]{2,1,0:T(8,128)S(1)}, f32[6,8,128]{2,1,0:T(8,128)S(1)}, u32[]{:S(2)}, u32[]{:S(2)}) collective-permute-start(f32[6,8,128]{2,1,0:T(8,128)S(1)} %get-tuple-element.20), channel_id=1, source_target_pairs={{16,0},{32,16},{48,32},{64,48},{80,64},{96,80},{112,96},{128,112},... | collective-permute-start | bytes 73736 | tf_op jit(solution)/shard_map/ppermute | solution.py:290

commit v2 on v0

v2 whole, which is shorter than its diff:
```python
import functools
import math

import jax
import jax.numpy as jnp
from jax import lax
from jax.experimental import pallas as pl
from jax.experimental.pallas import tpu as pltpu
from jax.sharding import PartitionSpec as P

F = 8192
STA = 128
GROUP = 128
LAGS = 6
PAIR_CAP = 3
TURNS = 3
STEP = 512
EPSILON = 1e-06
FROM_LEFT, FROM_RIGHT, LOCAL, REMOTE, DEAD = 0, 1, 2, 3, 4
CHUNKS = (1024, 2048, 1024)


def tables(first_bin, bin_count):
    turn = 1 + jnp.arange(TURNS, dtype=jnp.int32)
    bins = first_bin + jnp.arange(bin_count, dtype=jnp.int32)
    theta = (turn[:, None] * bins[None, :]).astype(jnp.float32) * jnp.float32(math.pi / F)
    return jnp.concatenate([jnp.cos(theta), jnp.sin(theta), jnp.zeros((2, bin_count), jnp.float32)])


def whiten(values):
    real, imag = values[0].astype(jnp.float32), values[1].astype(jnp.float32)
    power = real * real + imag * imag
    parts = []
    for start in range(0, power.shape[1], GROUP):
        energy = jnp.sum(power[:, start : start + GROUP], axis=1, keepdims=True) * (1.0 / (2 * GROUP))
        scale = lax.rsqrt(energy + EPSILON)
        parts.append(
            (
                (real[:, start : start + GROUP] * scale).astype(jnp.bfloat16),
                (imag[:, start : start + GROUP] * scale).astype(jnp.bfloat16),
            )
        )
    return jnp.concatenate([p[0] for p in parts], axis=1), jnp.concatenate([p[1] for p in parts], axis=1)


def put_parts(parts, real16, imag16, table):
    width = real16.shape[1]
    parts[:STA, :width] = real16
    parts[:STA, width:] = imag16
    real, imag = real16.astype(jnp.float32), imag16.astype(jnp.float32)
    for turn in range(TURNS):
        cos, sin = table[turn : turn + 1, :], table[TURNS + turn : TURNS + turn + 1, :]
        at = (1 + turn) * STA
        parts[at : at + STA, :width] = (real * cos).astype(jnp.bfloat16)
        parts[at : at + STA, width:] = (imag * cos).astype(jnp.bfloat16)
        at = (1 + TURNS + turn) * STA
        parts[at : at + STA, :width] = (imag * sin).astype(jnp.bfloat16)
        parts[at : at + STA, width:] = (real * -sin).astype(jnp.bfloat16)


def product(rows, columns):
    return lax.dot_general(rows, columns, (((1,), (1,)), ((), ())), preferred_element_type=jnp.float32)


PARTS = 2 * TURNS + 1
SUM_ROWS = PARTS * STA
SUMS = (2 * SUM_ROWS, 2 * STA)
TILE = LAGS * STA
OUT_ROWS = (PAIR_CAP + 2) * LAGS * 8


def lag_sum(sums, block, column, lag, first):
    turn = lag - LAGS // 2
    base = block * SUM_ROWS

    def part(index):
        row = base + index * STA
        row = row if isinstance(row, int) else pl.multiple_of(row, STA)
        return sums[pl.ds(row, STA), pl.ds(column, STA)]

    if turn == 0:
        return part(0)
    cosines, sines = part(abs(turn)), part(TURNS + abs(turn))
    return cosines - sines if (turn > 0) == first else cosines + sines


def whole(shape):
    return pl.BlockSpec(shape, lambda i, *_: (0,) * len(shape))


def params():
    return pltpu.CompilerParams(vmem_limit_bytes=60 << 20)


def cost(bins):
    return pl.CostEstimate(flops=2 * SUMS[0] * SUMS[1] * 2 * bins, bytes_accessed=8 << 20, transcendentals=0)


def slot_facts(pairs, count, slot):
    first_block = lax.axis_index("sta") * 2
    left, right = pairs[slot, 0] - first_block, pairs[slot, 1] - first_block
    kind = jnp.where(right == -1, FROM_LEFT, jnp.where(right == 2, FROM_RIGHT, LOCAL))
    kind = jnp.where((right == -2) | (right == 3), REMOTE, kind)
    return jnp.where(slot < count[0], kind, DEAD), left, right


def put_white(planes, white):
    real16, imag16 = whiten(planes)
    white[:, :STEP] = real16
    white[:, STEP:] = imag16


def split_kernel(raw, first, second, *white):
    planes = jnp.swapaxes(raw[0].astype(jnp.float32), 0, 1)
    plain = planes.astype(jnp.bfloat16)
    first[...] = plain[:, :STA]
    second[...] = plain[:, STA:]
    if white:
        put_white(planes, white[0])


def white_kernel(first, second, white):
    put_white(jnp.concatenate([first[...], second[...]], axis=1), white)


def plane_spec():
    return pl.BlockSpec((2, STA, STEP), lambda i, *_: (0, 0, i))


def white_spec():
    return pl.BlockSpec((2 * STA, 2 * STEP), lambda i, *_: (0, i))


def white_shape(count):
    return jax.ShapeDtypeStruct((2 * STA, 2 * count), jnp.bfloat16)


def split(raw_spectra, start, count, with_white):
    shape = jax.ShapeDtypeStruct((2, STA, count), jnp.bfloat16)
    return pl.pallas_call(
        split_kernel,
        out_shape=(shape, shape) + (white_shape(count),) * with_white,
        grid=(count // STEP,),
        in_specs=[pl.BlockSpec((1, 2 * STA, 2, STEP), lambda i: (0, 0, 0, start // STEP + i))],
        out_specs=(plane_spec(), plane_spec()) + (white_spec(),) * with_white,
        compiler_params=params(),
        cost_estimate=pl.CostEstimate(flops=0, bytes_accessed=24 * STA * count, transcendentals=0),
        name="split",
    )(raw_spectra)


def white_part(first, second):
    count = first.shape[2]
    return pl.pallas_call(
        white_kernel,
        out_shape=white_shape(count),
        grid=(count // STEP,),
        in_specs=[plane_spec(), plane_spec()],
        out_specs=white_spec(),
        compiler_params=params(),
        cost_estimate=pl.CostEstimate(flops=0, bytes_accessed=16 * STA * count, transcendentals=0),
        name="white",
    )(first, second)


def chunk_starts(chunks):
    starts = [0]
    for count in chunks:
        starts.append(starts[-1] + count // STEP)
    return starts


def local_kernel(starts, pairs, count, *refs):
    chunks = len(starts) - 1
    whites, (table_ref, local_ref, white, parts_first, parts_second, sums) = refs[:chunks], refs[chunks:]
    step = pl.program_id(0)
    last = pl.num_programs(0) - 1
    facts = [slot_facts(pairs, count, slot) for slot in range(PAIR_CAP)]
    here = [kind == LOCAL for kind, _, _ in facts]

    @pl.when(step == 0)
    def _():
        sums[...] = jnp.zeros_like(sums)

    for index in range(chunks):

        @pl.when((step >= starts[index]) & (step < starts[index + 1]))
        def _():
            white[...] = whites[index][...]

    table = table_ref[...]
    for block, parts in enumerate((parts_first, parts_second)):
        rows = white.at[block * STA : (block + 1) * STA, :]
        put_parts(parts, rows[:, :STEP], rows[:, STEP:], table)
    sums[:SUM_ROWS, :] += product(parts_first[...], white[...])
    sums[SUM_ROWS:, :] += product(parts_second[...], white[...])

    @pl.when(step == last)
    def _():
        for slot in range(PAIR_CAP):

            @pl.when(here[slot])
            def _():
                column = pl.multiple_of(facts[slot][2] * STA, STA)
                for lag in range(LAGS):
                    local_ref[slot, lag * STA : (lag + 1) * STA, :] = lag_sum(sums, facts[slot][1], column, lag, True)

            @pl.when(jnp.logical_not(here[slot]))
            def _():
                local_ref[slot] = jnp.zeros((TILE, STA), jnp.float32)


def local_part(pair_list, pair_count, whites, table):
    bins = table.shape[1]
    starts = chunk_starts([white.shape[1] // 2 for white in whites])

    def index(at, steps):
        return lambda i, *_: (0, jnp.clip(i - at, 0, steps - 1))

    specs = [
        pl.BlockSpec((2 * STA, 2 * STEP), index(starts[n], starts[n + 1] - starts[n])) for n in range(len(whites))
    ]
    return pl.pallas_call(
        functools.partial(local_kernel, tuple(starts)),
        out_shape=jax.ShapeDtypeStruct((PAIR_CAP, TILE, STA), jnp.float32),
        grid_spec=pltpu.PrefetchScalarGridSpec(
            num_scalar_prefetch=2,
            grid=(starts[-1],),
            in_specs=specs + [pl.BlockSpec((8, STEP), lambda i, *_: (0, i))],
            out_specs=whole((PAIR_CAP, TILE, STA)),
            scratch_shapes=[pltpu.VMEM((2 * STA, 2 * STEP), jnp.bfloat16)] + scratch(),
        ),
        compiler_params=params(),
        cost_estimate=cost(bins // 4),
        name="local_pairs",
    )(pair_list, pair_count, *whites, table)


def scratch():
    return [pltpu.VMEM((SUM_ROWS, 2 * STEP), jnp.bfloat16)] * 2 + [pltpu.VMEM(SUMS, jnp.float32)]


def accumulate(left, right, table_ref, white_ref, parts_left, parts_right, sums):
    table = table_ref[...]
    for source, parts in ((left, parts_left), (right, parts_right)):
        put_parts(parts, *whiten(source), table)
    sums[:SUM_ROWS, :] += product(parts_left[...], white_ref[...])
    sums[SUM_ROWS:, :] += product(parts_right[...], white_ref[...])


def early_kernel(left, right, table_ref, white_ref, *refs):
    before, (sums_ref, parts_left, parts_right) = refs[:-3], refs[-3:]

    @pl.when(pl.program_id(0) == 0)
    def _():
        sums_ref[...] = before[0][...] if before else jnp.zeros_like(sums_ref)

    accumulate(left, right, table_ref, white_ref, parts_left, parts_right, sums_ref)


def last_kernel(
    pairs, count, left, right, table_ref, white_ref, before, local, keep_ref, send_ref,
    parts_left, parts_right, sums, before_here, local_ref, arrived,
):
    step = pl.program_id(0)
    copies = (
        pltpu.make_async_copy(before, before_here, arrived.at[0]),
        pltpu.make_async_copy(local, local_ref, arrived.at[1]),
    )

    @pl.when(step == 0)
    def _():
        for copy in copies:
            copy.start()
        sums[...] = jnp.zeros_like(sums)

    accumulate(left, right, table_ref, white_ref, parts_left, parts_right, sums)

    @pl.when(step == pl.num_programs(0) - 1)
    def _():
        for copy in copies:
            copy.wait()
        sums[...] += before_here[...]
        even_core = lax.axis_index("band") == 0

        def put(place, tiles):
            octets = [tile.reshape(8, 2, 8, STA) for tile in tiles]
            even = jnp.concatenate([o[:, 0] for o in octets], axis=1)
            odd = jnp.concatenate([o[:, 1] for o in octets], axis=1)
            rows = slice(place * 8, place * 8 + 16)
            keep_ref[:, rows, :] = jnp.where(even_core, even, odd)
            send_ref[:, rows, :] = jnp.where(even_core, odd, even).astype(jnp.bfloat16)

        for slot in range(PAIR_CAP):
            kind, column_block, _ = slot_facts(pairs, count, slot)

            @pl.when(kind < LOCAL)
            def _():
                column = pl.multiple_of(column_block * STA, STA)
                for lag in range(0, LAGS, 2):
                    put(slot * LAGS + lag, [lag_sum(sums, kind, column, lag + n, False).T for n in range(2)])

            @pl.when(kind >= LOCAL)
            def _():
                for lag in range(0, LAGS, 2):
                    at = lag * STA
                    put(slot * LAGS + lag, [local_ref[slot, at + n * STA : at + (n + 1) * STA, :] for n in range(2)])

        for lag in range(0, LAGS, 2):
            put(PAIR_CAP * LAGS + lag, [lag_sum(sums, 1, 0, lag + n, True) for n in range(2)])
            put((PAIR_CAP + 1) * LAGS + lag, [lag_sum(sums, 0, STA, lag + n, True) for n in range(2)])


def early_part(left, right, white, table, start, *before):
    bins = left.shape[2]
    base = start // STEP
    return pl.pallas_call(
        early_kernel,
        out_shape=jax.ShapeDtypeStruct(SUMS, jnp.float32),
        grid=(bins // STEP,),
        in_specs=[
            plane_spec(),
            plane_spec(),
            pl.BlockSpec((8, STEP), lambda i: (0, base + i)),
            white_spec(),
        ]
        + [whole(SUMS)] * len(before),
        out_specs=whole(SUMS),
        scratch_shapes=scratch()[:2],
        compiler_params=params(),
        cost_estimate=cost(bins),
        name="early_pairs",
    )(left, right, table, white, *before)


def last_part(pair_list, pair_count, left, right, white, table, before, local):
    bins = left.shape[2]
    base = (table.shape[1] - bins) // STEP
    result = (8, OUT_ROWS, STA)
    there = pl.BlockSpec(memory_space=pl.ANY)
    return pl.pallas_call(
        last_kernel,
        out_shape=(jax.ShapeDtypeStruct(result, jnp.float32), jax.ShapeDtypeStruct(result, jnp.bfloat16)),
        grid_spec=pltpu.PrefetchScalarGridSpec(
            num_scalar_prefetch=2,
            grid=(bins // STEP,),
            in_specs=[
                plane_spec(),
                plane_spec(),
                pl.BlockSpec((8, STEP), lambda i, *_: (0, base + i)),
                white_spec(),
                there,
                there,
            ],
            out_specs=(whole(result), whole(result)),
            scratch_shapes=scratch()
            + [
                pltpu.VMEM(SUMS, jnp.float32),
                pltpu.VMEM(local.shape, jnp.float32),
                pltpu.SemaphoreType.DMA((2,)),
            ],
        ),
        compiler_params=params(),
        cost_estimate=cost(bins),
        name="last_pairs",
    )(pair_list, pair_count, left, right, table, white, before, local)


def body(raw_spectra, pair_list, pair_count):
    bins_dev = raw_spectra.shape[3]
    sta_count = lax.axis_size("sta")
    position = lax.axis_index("sta")
    core = lax.axis_index("band")
    to_right = [(i, i + 1) for i in range(sta_count - 1)]
    to_left = [(i + 1, i) for i in range(sta_count - 1)]

    def send(pair):
        return lax.ppermute(pair[1], "sta", to_right), lax.ppermute(pair[0], "sta", to_left)

    planes = []
    received = []
    start = 0
    rest = raw_spectra
    for index, count in enumerate(CHUNKS):
        first, second, *white = split(rest, start, count, int(index > 0))
        planes.append((first, second, white))
        if index + 1 < len(CHUNKS):
            received.append(send((first, second)))
            first, second, rest = lax.optimization_barrier((first, second, rest))
        start += count
    table = tables(core * bins_dev, bins_dev)
    head, received[0] = lax.optimization_barrier((planes[0][:2], received[0]))
    whites = [white_part(*head)] + [white[0] for _, _, white in planes[1:]]
    ending, whites[0], table = lax.optimization_barrier((planes[-1][:2], whites[0], table))
    received.append(send(ending))
    right_id = pair_list[:, 1] - position * 2
    live = jnp.arange(PAIR_CAP) < pair_count[0]
    local = lax.cond(
        jnp.any(live & (right_id >= 0) & (right_id <= 1)),
        lambda: local_part(pair_list, pair_count, whites, table),
        lambda: jnp.zeros((PAIR_CAP, TILE, STA), jnp.float32),
    )
    before = ()
    start = 0
    for count, pair, white in zip(CHUNKS[:-1], received[:-1], whites[:-1]):
        before = (early_part(*pair, white, table, start, *before),)
        start += count
    keep, send = last_part(pair_list, pair_count, *received[-1], whites[-1], table, *before, local)

    other = lax.ppermute(send, "band", [(0, 1), (1, 0)])
    pieces = (keep + other.astype(jnp.float32)).astype(jnp.bfloat16)
    gathered = lax.all_to_all(pieces, "seg", 0, 0)
    scale = jnp.float32(1.0 / math.sqrt(F * raw_spectra.shape[0] * lax.axis_size("seg")))
    totals = jnp.sum(gathered.astype(jnp.float32), axis=0) * scale
    totals = totals.reshape(PAIR_CAP + 2, LAGS, 8, STA)
    going_right = totals[PAIR_CAP]
    from_left = lax.ppermute(going_right, "sta", to_right)
    totals, going_right = lax.optimization_barrier((totals, going_right))
    from_right = lax.ppermute(totals[PAIR_CAP + 1], "sta", to_left)
    remote = (live & ((right_id == -2) | (right_id == 3)))[:, None, None, None]
    is_left = (right_id < 0)[:, None, None, None]
    return jnp.where(remote, jnp.where(is_left, from_left[None], from_right[None]), totals[:PAIR_CAP])


def solution(mesh):
    in_specs = (P("seg", "sta", None, "band"), P("sta", None), P("sta"))
    out_specs = P("sta", None, ("seg", "band"), None)
    return jax.shard_map(body, mesh=mesh, in_specs=in_specs, out_specs=out_specs, check_vma=False)
```

time: 246 us -> 110 us (0.45)
  waiting for transfers between devices: 156 us -> 6.93 us
  other arithmetic: 40.5 us -> 3.4 us
  Pallas kernels: 0 us -> 32.3 us
  starting transfers between devices: 13.1 us -> 39.4 us
  blocking collectives: 0 us -> 24 us
  between operations: 14.2 us -> 1.47 us
  matrix products: 10.2 us -> 0 us
  local copies, waits for them, and re-layouts: 8.84 us -> 1.65 us
  loops' own time: 2.84 us -> 0.02 us
    ppermute x2 -> x9, waiting for transfers between devices: 93.2 us -> 6.93 us  [the longest x3 2.66 us: send(): lax.ppermute(pair[0], 'sta', to_left)]
    reduce_scatter x1 -> x0, waiting for transfers between devices: 62.9 us -> none  [body(): lax.psum_scatter(jnp.stack(own_terms), ('seg', 'band'), scatter_dimension...]
    pallas_call x0 -> x7, Pallas kernels: none -> 32.3 us  [the longest x2 13 us: early_part(): pl.pallas_call(early_kernel, out_shape=jax.ShapeDtypeStruct(SUMS, jnp.flo...]
    ppermute x2 -> x9, starting transfers between devices: 13.1 us -> 39.4 us  [the longest x3 20.9 us: send(): lax.ppermute(pair[0], 'sta', to_left)]
    all_to_all x0 -> x1, blocking collectives: none -> 24 us  [body(): gathered = lax.all_to_all(pieces, 'seg', 0, 0)]
    concatenate x1, other arithmetic: 10.4 us -> 0.08 us  [tables(): jnp.concatenate([jnp.cos(theta), jnp.sin(theta), jnp.zeros((2, bin_count)...]
    dot_general x2 -> x0, matrix products: 10.2 us -> none  [pair_term(): lax.dot_general(rotated, right_flat, (((1, 3), (0, 2)), ((), ())), prefer...]
    reduce_sum x2 -> x1, other arithmetic: 10.1 us -> 0.07 us  [body(): totals = jnp.sum(gathered.astype(jnp.float32), axis=0) * scale]
  transfers between devices with their start and end apart: 3 -> 9, of which waited for: 3 -> 6; matrix products, arithmetic and copies ran while one was open for 0% -> 2% of each run, Pallas kernels for 0% -> 22%
where the time goes in v2:
time: 110 us; the launch traced here: 109 us
  starting transfers between devices  39.4 us (36%)
  Pallas kernels  32.3 us (29%)
  blocking collectives  24 us (22%)
  waiting for transfers between devices  6.93 us (6%)
  other arithmetic  3.4 us (3%)
  local copies, waits for them, and re-layouts  1.65 us (2%)
  between operations  1.47 us (1%)
    all_to_all x1, blocking collectives, body(): gathered = lax.all_to_all(pieces, 'seg', 0, 0)  24 us
    ppermute x3, starting transfers between devices, send(): lax.ppermute(pair[0], 'sta', to_left)  20.9 us
    pallas_call x2, Pallas kernels, early_part(): pl.pallas_call(early_kernel, out_shape=jax.ShapeDtypeStruct(SUMS, jnp.flo...  13 us
    pallas_call x3, Pallas kernels, split(): pl.pallas_call(split_kernel, out_shape=(shape, shape) + (white_shape(coun...  11.4 us
    ppermute x3, starting transfers between devices, send(): lax.ppermute(pair[1], 'sta', to_right)  8.1 us
    ppermute x1, starting transfers between devices, body(): from_right = lax.ppermute(totals[PAIR_CAP + 1], 'sta', to_left)  6.5 us
    pallas_call x1, Pallas kernels, last_part(): pl.pallas_call(last_kernel, out_shape=(jax.ShapeDtypeStruct(result, jnp.f...  6.35 us
    ppermute x3, waiting for transfers between devices, send(): lax.ppermute(pair[0], 'sta', to_left)  2.66 us
  transfers between devices with their start and end apart: 9, of which 6 were waited for; matrix products, arithmetic and copies ran while one was open for 2% of the time, Pallas kernels for 22%

profile of v2, /device:TPU:6, one launch (start us, length us, event | category | flops | bytes accessed | tf_op | source)
XLA Modules:
  0.0 109.2 jit_solution(3283040677664118287)
XLA Ops:
  0.0 2.3 %split.3 = (bf16[2,128,1024]{2,1,0:T(8,128)(2,1)}, bf16[2,128,1024]{2,1,0:T(8,128)(2,1)}) custom-call(bf16[1,256,2,4096]{3,2,1,0:T(2,128)(2,1)} %raw.3), custom_call_target="tpu_custom_call" | custom-call | bytes 3145728 | tf_op jit(solution)/shard_map/split/pallas_call | solution.py:140
  2.3 4.3 %collective-permute-start = (bf16[2,128,1024]{2,1,0:T(8,128)(2,1)}, bf16[2,128,1024]{2,1,0:T(8,128)(2,1)S(1)}, u32[]{:S(2)}, u32[]{:S(2)}) collective-permute-start(bf16[2,128,1024]{2,1,0:T(8,128)(2,1)} %get-tuple-element.56.second), channel_id=1, source_target_pairs={{0,16},{16,32},{32,48},{48,64},{64,80},{80,96},{96,112},{112,128},... | collective-permute-start | bytes 1572872 | tf_op jit(solution)/shard_map/ppermute | solution.py:378
  6.6 8.9 %collective-permute-start.1 = (bf16[2,128,1024]{2,1,0:T(8,128)(2,1)}, bf16[2,128,1024]{2,1,0:T(8,128)(2,1)}, u32[]{:S(2)}, u32[]{:S(2)}) collective-permute-start(bf16[2,128,1024]{2,1,0:T(8,128)(2,1)} %get-tuple-element.55.first), channel_id=1, source_target_pairs={{16,0},{32,16},{48,32},{64,48},{80,64},{96,80},{112,96},{128,112},... | collective-permute-start | bytes 1572872 | tf_op jit(solution)/shard_map/ppermute | solution.py:378
  15.4 6.0 %split.4 = (bf16[2,128,2048]{2,1,0:T(8,128)(2,1)}, bf16[2,128,2048]{2,1,0:T(8,128)(2,1)}, bf16[256,4096]{1,0:T(8,128)(2,1)}) custom-call(bf16[1,256,2,4096]{3,2,1,0:T(2,128)(2,1)} %raw.3), custom_call_target="tpu_custom_call" | custom-call | bytes 6291456 | tf_op jit(solution)/shard_map/split/pallas_call | solution.py:140
  21.4 1.9 %collective-permute-start.4 = (bf16[2,128,2048]{2,1,0:T(8,128)(2,1)}, bf16[2,128,2048]{2,1,0:T(8,128)(2,1)}, u32[]{:S(2)}, u32[]{:S(2)}) collective-permute-start(bf16[2,128,2048]{2,1,0:T(8,128)(2,1)} %get-tuple-element.51), channel_id=1, source_target_pairs={{0,16},{16,32},{32,48},{48,64},{64,80},{80,96},{96,112},{112,128},... | collective-permute-start | bytes 3145736 | tf_op jit(solution)/shard_map/ppermute | solution.py:378
  23.4 6.0 %collective-permute-start.5 = (bf16[2,128,2048]{2,1,0:T(8,128)(2,1)}, bf16[2,128,2048]{2,1,0:T(8,128)(2,1)}, u32[]{:S(2)}, u32[]{:S(2)}) collective-permute-start(bf16[2,128,2048]{2,1,0:T(8,128)(2,1)} %get-tuple-element.50), channel_id=1, source_target_pairs={{16,0},{32,16},{48,32},{64,48},{80,64},{96,80},{112,96},{128,112},... | collective-permute-start | bytes 3145736 | tf_op jit(solution)/shard_map/ppermute | solution.py:378
  29.4 0.7 copy.5.pairs
  30.7 3.1 %split.5 = (bf16[2,128,1024]{2,1,0:T(8,128)(2,1)}, bf16[2,128,1024]{2,1,0:T(8,128)(2,1)}, bf16[256,2048]{1,0:T(8,128)(2,1)S(1)}) custom-call(bf16[1,256,2,4096]{3,2,1,0:T(2,128)(2,1)} %raw.3), custom_call_target="tpu_custom_call" | custom-call | bytes 3145728 | tf_op jit(solution)/shard_map/split/pallas_call | solution.py:140
  33.8 0.6 bitcast_and_fusion.2
  35.1 0.5 fusion.1
  35.8 0.1 maximum_maximum_fusion.table_ref
  35.9 0.8 copy-done.1
  36.7 1.6 %white.1.white_ref = bf16[256,2048]{1,0:T(8,128)(2,1)S(1)} custom-call(bf16[2,128,1024]{2,1,0:T(8,128)(2,1)} %get-tuple-element.55.first, bf16[2,128,1024]{2,1,0:T(8,128)(2,1)} %get-tuple-element.56.second), custom_call_target="tpu_custom_call" | custom-call | bytes 2097152 | tf_op jit(solution)/shard_map/white/pallas_call | solution.py:154
  38.3 1.9 %collective-permute-start.2 = (bf16[2,128,1024]{2,1,0:T(8,128)(2,1)}, bf16[2,128,1024]{2,1,0:T(8,128)(2,1)}, u32[]{:S(2)}, u32[]{:S(2)}) collective-permute-start(bf16[2,128,1024]{2,1,0:T(8,128)(2,1)} %get-tuple-element.57), channel_id=1, source_target_pairs={{0,16},{16,32},{32,48},{48,64},{64,80},{80,96},{96,112},{112,128},... | collective-permute-start | bytes 1572872 | tf_op jit(solution)/shard_map/ppermute | solution.py:378
  40.2 6.0 %collective-permute-start.3 = (bf16[2,128,1024]{2,1,0:T(8,128)(2,1)}, bf16[2,128,1024]{2,1,0:T(8,128)(2,1)}, u32[]{:S(2)}, u32[]{:S(2)}) collective-permute-start(bf16[2,128,1024]{2,1,0:T(8,128)(2,1)} %get-tuple-element.58), channel_id=1, source_target_pairs={{16,0},{32,16},{48,32},{64,48},{80,64},{96,80},{112,96},{128,112},... | collective-permute-start | bytes 1572872 | tf_op jit(solution)/shard_map/ppermute | solution.py:378
  46.2 0.1 conditional.1
  46.3 0.1 broadcast.58
  46.4 4.8 %early_pairs.2.refs_0_ = f32[1792,256]{1,0:T(8,128)} custom-call(bf16[2,128,1024]{2,1,0:T(8,128)(2,1)} %copy-done.1, bf16[2,128,1024]{2,1,0:T(8,128)(2,1)} %collective-permute-done.1.right, f32[8,4096]{1,0:T(8,128)S(1)} %maximum_maximum_fusion.table_ref, bf16[256,2048]{1,0:T(8,128)(2,1)S(1)} %white.1.white_ref), custom_call_target="tpu_custom_call" | custom-call | flops 1879048192 | bytes 8388608 | tf_op jit(solution)/shard_map/early_pairs/pallas_call | solution.py:317
  51.2 0.7 collective-permute-done.4.left
  51.8 1.5 %collective-permute-done.5.right = bf16[2,128,2048]{2,1,0:T(8,128)(2,1)} collective-permute-done((bf16[2,128,2048]{2,1,0:T(8,128)(2,1)}, bf16[2,128,2048]{2,1,0:T(8,128)(2,1)}, u32[]{:S(2)}, u32[]{:S(2)}) %collective-permute-start.5) | collective-permute-done | bytes 1048608 | tf_op jit(solution)/shard_map/ppermute | solution.py:378
  53.3 8.2 %early_pairs.3.before = f32[1792,256]{1,0:T(8,128)} custom-call(bf16[2,128,2048]{2,1,0:T(8,128)(2,1)} %collective-permute-done.4.left, bf16[2,128,2048]{2,1,0:T(8,128)(2,1)} %collective-permute-done.5.right, f32[8,4096]{1,0:T(8,128)S(1)} %maximum_maximum_fusion.table_ref, bf16[256,4096]{1,0:T(8,128)(2,1)} %get-tuple-element.61.white_ref, ...), custom_call_target="tpu_custom_call" | custom-call | flops 3758096384 | bytes 8388608 | tf_op jit(solution)/shard_map/early_pairs/pallas_call | solution.py:317
  61.5 0.1 collective-permute-done.2.left
  61.6 1.2 %collective-permute-done.3.right = bf16[2,128,1024]{2,1,0:T(8,128)(2,1)} collective-permute-done((bf16[2,128,1024]{2,1,0:T(8,128)(2,1)}, bf16[2,128,1024]{2,1,0:T(8,128)(2,1)}, u32[]{:S(2)}, u32[]{:S(2)}) %collective-permute-start.3) | collective-permute-done | bytes 524320 | tf_op jit(solution)/shard_map/ppermute | solution.py:378
  62.8 6.3 %last_pairs.1 = (f32[8,240,128]{2,1,0:T(8,128)}, bf16[8,240,128]{2,1,0:T(8,128)(2,1)}) custom-call(s32[3,2]{1,0:T(4,128)} %copy.5.pairs, s32[1]{0:T(128)} %copy.8.count, bf16[2,128,1024]{2,1,0:T(8,128)(2,1)} %collective-permute-done.2.left, bf16[2,128,1024]{2,1,0:T(8,128)(2,1)} %collective-permute-done.3.right, f32[8,4096]{1,0:T(8,128)S(1)} %maximum_maximum_fusion.table_ref, ...), custom_call_target="tpu_custom_call" | custom-call | flops 1879048192 | bytes 8388608 | tf_op jit(solution)/shard_map/last_pairs/pallas_call | solution.py:341
  69.1 1.9 %collective-permute-start.6 = (bf16[8,240,128]{2,1,0:T(8,128)(2,1)}, bf16[8,240,128]{2,1,0:T(8,128)(2,1)S(1)}, u32[]{:S(2)}, u32[]{:S(2)}) collective-permute-start(bf16[8,240,128]{2,1,0:T(8,128)(2,1)} %get-tuple-element.66), channel_id=1, source_target_pairs={{0,1},{1,0},{2,3},{3,2},{4,5},{5,4},{6,7},{7,6},{8,9},{9,8},{10,11... | collective-permute-start | bytes 1474568 | tf_op jit(solution)/shard_map/ppermute | solution.py:410
  71.1 2.0 %collective-permute-done.6 = bf16[8,240,128]{2,1,0:T(8,128)(2,1)S(1)} collective-permute-done((bf16[8,240,128]{2,1,0:T(8,128)(2,1)}, bf16[8,240,128]{2,1,0:T(8,128)(2,1)S(1)}, u32[]{:S(2)}, u32[]{:S(2)}) %collective-permute-start.6) | collective-permute-done | bytes 491552 | tf_op jit(solution)/shard_map/ppermute | solution.py:410
  73.1 1.3 %add_convert_fusion = bf16[8,240,128]{2,1,0:T(8,128)(2,1)S(1)} fusion(f32[8,240,128]{2,1,0:T(8,128)} %get-tuple-element.65, bf16[8,240,128]{2,1,0:T(8,128)(2,1)S(1)} %collective-permute-done.6), kind=kLoop, calls=%fused_computation.1 | loop fusion | flops 737280 | bytes 1966080 | tf_op jit(solution)/shard_map/convert_element_type | solution.py:411
  74.4 24.0 %all_to_all.5 = bf16[8,240,128]{2,1,0:T(8,128)(2,1)S(1)} all-to-all(bf16[8,240,128]{2,1,0:T(8,128)(2,1)S(1)} %add_convert_fusion), channel_id=1, replica_groups=mesh['sta'=32,'seg'=8,'band'=2] {'seg'}, dimensions={0} | all-to-all | bytes 983040 | tf_op jit(solution)/shard_map/all_to_all | solution.py:412
  98.5 1.9 %collective-permute-start.7 = (f32[6,8,128]{2,1,0:T(8,128)S(1)}, f32[6,8,128]{2,1,0:T(8,128)S(1)}, u32[]{:S(2)}, u32[]{:S(2)}) collective-permute-start(f32[6,8,128]{2,1,0:T(8,128)S(1)} %slice_bitcast_fusion), channel_id=1, source_target_pairs={{0,16},{16,32},{32,48},{48,64},{64,80},{80,96},{96,112},{112,128},... | collective-permute-start | bytes 73736 | tf_op jit(solution)/shard_map/ppermute | solution.py:417
  100.5 6.5 %collective-permute-start.8 = (f32[6,8,128]{2,1,0:T(8,128)S(1)}, f32[6,8,128]{2,1,0:T(8,128)S(1)}, u32[]{:S(2)}, u32[]{:S(2)}) collective-permute-start(f32[6,8,128]{2,1,0:T(8,128)S(1)} %slice_bitcast_fusion.1), channel_id=1, source_target_pairs={{16,0},{32,16},{48,32},{64,48},{80,64},{96,80},{112,96},{128,112},... | collective-permute-start | bytes 73736 | tf_op jit(solution)/shard_map/ppermute | solution.py:419
  107.0 1.5 %collective-permute-done.8 = f32[6,8,128]{2,1,0:T(8,128)S(1)} collective-permute-done((f32[6,8,128]{2,1,0:T(8,128)S(1)}, f32[6,8,128]{2,1,0:T(8,128)S(1)}, u32[]{:S(2)}, u32[]{:S(2)}) %collective-permute-start.8) | collective-permute-done | bytes 24608 | tf_op jit(solution)/shard_map/ppermute | solution.py:419
  108.5 0.7 slice_select_fusion
  (15 shorter events, 0.2 us)
Async XLA Ops:
  2.3 33.6 %collective-permute-start = (bf16[2,128,1024]{2,1,0:T(8,128)(2,1)}, bf16[2,128,1024]{2,1,0:T(8,128)(2,1)S(1)}, u32[]{:S(2)}, u32[]{:S(2)}) collective-permute-start(bf16[2,128,1024]{2,1,0:T(8,128)(2,1)} %get-tuple-element.56.second), channel_id=1, source_target_pairs={{0,16},{16,32},{32,48},{48,64},{64,80},{80,96},{96,112},{112,128},... | collective-permute-start | bytes 1572872 | tf_op jit(solution)/shard_map/ppermute | solution.py:378
  6.5 22.9 %copy-start = (s32[3,2]{0,1:T(2,128)S(1)}, s32[3,2]{0,1:T(2,128)}, u32[]{:S(2)}) copy-start(s32[3,2]{0,1:T(2,128)} %param.6) | copy-start | bytes 76
  6.6 30.1 %collective-permute-start.1 = (bf16[2,128,1024]{2,1,0:T(8,128)(2,1)}, bf16[2,128,1024]{2,1,0:T(8,128)(2,1)}, u32[]{:S(2)}, u32[]{:S(2)}) collective-permute-start(bf16[2,128,1024]{2,1,0:T(8,128)(2,1)} %get-tuple-element.55.first), channel_id=1, source_target_pairs={{16,0},{32,16},{48,32},{64,48},{80,64},{96,80},{112,96},{128,112},... | collective-permute-start | bytes 1572872 | tf_op jit(solution)/shard_map/ppermute | solution.py:378
  21.4 30.4 %collective-permute-start.4 = (bf16[2,128,2048]{2,1,0:T(8,128)(2,1)}, bf16[2,128,2048]{2,1,0:T(8,128)(2,1)}, u32[]{:S(2)}, u32[]{:S(2)}) collective-permute-start(bf16[2,128,2048]{2,1,0:T(8,128)(2,1)} %get-tuple-element.51), channel_id=1, source_target_pairs={{0,16},{16,32},{32,48},{48,64},{64,80},{80,96},{96,112},{112,128},... | collective-permute-start | bytes 3145736 | tf_op jit(solution)/shard_map/ppermute | solution.py:378
  23.4 30.0 %collective-permute-start.5 = (bf16[2,128,2048]{2,1,0:T(8,128)(2,1)}, bf16[2,128,2048]{2,1,0:T(8,128)(2,1)}, u32[]{:S(2)}, u32[]{:S(2)}) collective-permute-start(bf16[2,128,2048]{2,1,0:T(8,128)(2,1)} %get-tuple-element.50), channel_id=1, source_target_pairs={{16,0},{32,16},{48,32},{64,48},{80,64},{96,80},{112,96},{128,112},... | collective-permute-start | bytes 3145736 | tf_op jit(solution)/shard_map/ppermute | solution.py:378
  35.9 0.8 copy-start.1
  38.3 23.3 %collective-permute-start.2 = (bf16[2,128,1024]{2,1,0:T(8,128)(2,1)}, bf16[2,128,1024]{2,1,0:T(8,128)(2,1)}, u32[]{:S(2)}, u32[]{:S(2)}) collective-permute-start(bf16[2,128,1024]{2,1,0:T(8,128)(2,1)} %get-tuple-element.57), channel_id=1, source_target_pairs={{0,16},{16,32},{32,48},{48,64},{64,80},{80,96},{96,112},{112,128},... | collective-permute-start | bytes 1572872 | tf_op jit(solution)/shard_map/ppermute | solution.py:378
  40.2 22.6 %collective-permute-start.3 = (bf16[2,128,1024]{2,1,0:T(8,128)(2,1)}, bf16[2,128,1024]{2,1,0:T(8,128)(2,1)}, u32[]{:S(2)}, u32[]{:S(2)}) collective-permute-start(bf16[2,128,1024]{2,1,0:T(8,128)(2,1)} %get-tuple-element.58), channel_id=1, source_target_pairs={{16,0},{32,16},{48,32},{64,48},{80,64},{96,80},{112,96},{128,112},... | collective-permute-start | bytes 1572872 | tf_op jit(solution)/shard_map/ppermute | solution.py:378
  69.1 4.0 %collective-permute-start.6 = (bf16[8,240,128]{2,1,0:T(8,128)(2,1)}, bf16[8,240,128]{2,1,0:T(8,128)(2,1)S(1)}, u32[]{:S(2)}, u32[]{:S(2)}) collective-permute-start(bf16[8,240,128]{2,1,0:T(8,128)(2,1)} %get-tuple-element.66), channel_id=1, source_target_pairs={{0,1},{1,0},{2,3},{3,2},{4,5},{5,4},{6,7},{7,6},{8,9},{9,8},{10,11... | collective-permute-start | bytes 1474568 | tf_op jit(solution)/shard_map/ppermute | solution.py:410
  98.5 9.9 %collective-permute-start.7 = (f32[6,8,128]{2,1,0:T(8,128)S(1)}, f32[6,8,128]{2,1,0:T(8,128)S(1)}, u32[]{:S(2)}, u32[]{:S(2)}) collective-permute-start(f32[6,8,128]{2,1,0:T(8,128)S(1)} %slice_bitcast_fusion), channel_id=1, source_target_pairs={{0,16},{16,32},{32,48},{48,64},{64,80},{80,96},{96,112},{112,128},... | collective-permute-start | bytes 73736 | tf_op jit(solution)/shard_map/ppermute | solution.py:417
  100.5 8.0 %collective-permute-start.8 = (f32[6,8,128]{2,1,0:T(8,128)S(1)}, f32[6,8,128]{2,1,0:T(8,128)S(1)}, u32[]{:S(2)}, u32[]{:S(2)}) collective-permute-start(f32[6,8,128]{2,1,0:T(8,128)S(1)} %slice_bitcast_fusion.1), channel_id=1, source_target_pairs={{16,0},{32,16},{48,32},{64,48},{80,64},{96,80},{112,96},{128,112},... | collective-permute-start | bytes 73736 | tf_op jit(solution)/shard_map/ppermute | solution.py:419

commit v3 on v2

--- a/solution.py
+++ b/solution.py
@@ -17,7 +17,7 @@
 STEP = 512
 EPSILON = 1e-06
 FROM_LEFT, FROM_RIGHT, LOCAL, REMOTE, DEAD = 0, 1, 2, 3, 4
-CHUNKS = (1024, 2048, 1024)
+CHUNKS = (1536, 1536, 1024)
 
 
 def tables(first_bin, bin_count):
@@ -287,7 +287,7 @@
             octets = [tile.reshape(8, 2, 8, STA) for tile in tiles]
             even = jnp.concatenate([o[:, 0] for o in octets], axis=1)
             odd = jnp.concatenate([o[:, 1] for o in octets], axis=1)
-            rows = slice(place * 8, place * 8 + 16)
+            rows = pl.ds(place * 8 if isinstance(place, int) else pl.multiple_of(place * 8, 16), 16)
             keep_ref[:, rows, :] = jnp.where(even_core, even, odd)
             send_ref[:, rows, :] = jnp.where(even_core, odd, even).astype(jnp.bfloat16)
 
@@ -306,9 +306,11 @@
                     at = lag * STA
                     put(slot * LAGS + lag, [local_ref[slot, at + n * STA : at + (n + 1) * STA, :] for n in range(2)])
 
-        for lag in range(0, LAGS, 2):
-            put(PAIR_CAP * LAGS + lag, [lag_sum(sums, 1, 0, lag + n, True) for n in range(2)])
-            put((PAIR_CAP + 1) * LAGS + lag, [lag_sum(sums, 0, STA, lag + n, True) for n in range(2)])
+        odd_place = lax.axis_index("sta") % 2
+        for side, (block, column) in enumerate(((1, 0), (0, STA))):
+            base = (PAIR_CAP + (odd_place + side) % 2) * LAGS
+            for lag in range(0, LAGS, 2):
+                put(base + lag, [lag_sum(sums, block, column, lag + n, True) for n in range(2)])
 
 
 def early_part(left, right, white, table, start, *before):
@@ -391,7 +393,8 @@
     table = tables(core * bins_dev, bins_dev)
     head, received[0] = lax.optimization_barrier((planes[0][:2], received[0]))
     whites = [white_part(*head)] + [white[0] for _, _, white in planes[1:]]
-    ending, whites[0], table = lax.optimization_barrier((planes[-1][:2], whites[0], table))
+    before = early_part(*received[0], whites[0], table, 0)
+    ending, before = lax.optimization_barrier((planes[-1][:2], before))
     received.append(send(ending))
     right_id = pair_list[:, 1] - position * 2
     live = jnp.arange(PAIR_CAP) < pair_count[0]
@@ -400,26 +403,32 @@
         lambda: local_part(pair_list, pair_count, whites, table),
         lambda: jnp.zeros((PAIR_CAP, TILE, STA), jnp.float32),
     )
-    before = ()
-    start = 0
-    for count, pair, white in zip(CHUNKS[:-1], received[:-1], whites[:-1]):
-        before = (early_part(*pair, white, table, start, *before),)
+    start = CHUNKS[0]
+    for count, pair, white in zip(CHUNKS[1:-1], received[1:-1], whites[1:-1]):
+        before = early_part(*pair, white, table, start, before)
         start += count
-    keep, send = last_part(pair_list, pair_count, *received[-1], whites[-1], table, *before, local)
-
-    other = lax.ppermute(send, "band", [(0, 1), (1, 0)])
-    pieces = (keep + other.astype(jnp.float32)).astype(jnp.bfloat16)
-    gathered = lax.all_to_all(pieces, "seg", 0, 0)
+    keep, send_half = last_part(pair_list, pair_count, *received[-1], whites[-1], table, before, local)
+
+    other = lax.ppermute(send_half, "band", [(0, 1), (1, 0)])
+    own_rows = PAIR_CAP * LAGS * 8
+
+    def summed(start, count):
+        rows = slice(start, start + count)
+        return (keep[:, rows] + other[:, rows].astype(jnp.float32)).astype(jnp.bfloat16)
+
+    swap_even = [(i, i ^ 1) for i in range(sta_count)]
+    swap_odd = [(i, ((i + 1) ^ 1) - 1) for i in range(1, sta_count - 1)]
+    foreign = summed(own_rows, 2 * LAGS * 8)
+    got_even = lax.ppermute(foreign[:, : LAGS * 8], "sta", swap_even)
+    got_odd = lax.ppermute(foreign[:, LAGS * 8 :], "sta", swap_odd)
+    far = (live & ((right_id == -2) | (right_id == 3)))[None, :, None, None]
+    over_even = ((right_id < 0) == (position % 2 == 1))[None, :, None, None]
+    own = summed(0, own_rows).reshape(8, PAIR_CAP, LAGS * 8, STA)
+    pieces = jnp.where(far, jnp.where(over_even, got_even[:, None], got_odd[:, None]), own)
+    gathered = lax.all_to_all(pieces.reshape(8, own_rows, STA), "seg", 0, 0)
     scale = jnp.float32(1.0 / math.sqrt(F * raw_spectra.shape[0] * lax.axis_size("seg")))
     totals = jnp.sum(gathered.astype(jnp.float32), axis=0) * scale
-    totals = totals.reshape(PAIR_CAP + 2, LAGS, 8, STA)
-    going_right = totals[PAIR_CAP]
-    from_left = lax.ppermute(going_right, "sta", to_right)
-    totals, going_right = lax.optimization_barrier((totals, going_right))
-    from_right = lax.ppermute(totals[PAIR_CAP + 1], "sta", to_left)
-    remote = (live & ((right_id == -2) | (right_id == 3)))[:, None, None, None]
-    is_left = (right_id < 0)[:, None, None, None]
-    return jnp.where(remote, jnp.where(is_left, from_left[None], from_right[None]), totals[:PAIR_CAP])
+    return totals.reshape(PAIR_CAP, LAGS, 8, STA)
 
 
 def solution(mesh):

time: 110 us -> 113 us (1.027)
  the two profiles are of different devices: /device:TPU:6 before, /device:TPU:196 now
where the time goes in v3:
time: 113 us; the launch traced here: 112 us
  starting transfers between devices  40 us (35%)
  Pallas kernels  34.7 us (31%)
  blocking collectives  19.3 us (17%)
  waiting for transfers between devices  12.1 us (11%)
  other arithmetic  3.21 us (3%)
  between operations  1.52 us (1%)
  local copies, waits for them, and re-layouts  1.18 us (1%)
    all_to_all x1, blocking collectives, body(): gathered = lax.all_to_all(pieces.reshape(8, own_rows, STA), 'seg', 0, 0)  19.3 us
    ppermute x1, starting transfers between devices, body(): got_odd = lax.ppermute(foreign[:, LAGS * 8:], 'sta', swap_odd)  15.7 us
    pallas_call x2, Pallas kernels, early_part(): pl.pallas_call(early_kernel, out_shape=jax.ShapeDtypeStruct(SUMS, jnp.flo...  13.1 us
    ppermute x3, starting transfers between devices, send(): lax.ppermute(pair[1], 'sta', to_right)  12.8 us
    pallas_call x3, Pallas kernels, split(): pl.pallas_call(split_kernel, out_shape=(shape, shape) + (white_shape(coun...  12.4 us
    ppermute x3, starting transfers between devices, send(): lax.ppermute(pair[0], 'sta', to_left)  7.51 us
    ppermute x3, waiting for transfers between devices, send(): lax.ppermute(pair[0], 'sta', to_left)  7.35 us
    pallas_call x1, Pallas kernels, last_part(): pl.pallas_call(last_kernel, out_shape=(jax.ShapeDtypeStruct(result, jnp.f...  6.3 us
  transfers between devices with their start and end apart: 9, of which 4 were waited for; matrix products, arithmetic and copies ran while one was open for 2% of the time, Pallas kernels for 22%

profile of v3, /device:TPU:196, one launch (start us, length us, event | category | flops | bytes accessed | tf_op | source)
XLA Modules:
  0.0 112.0 jit_solution(11051249049750212325)
XLA Ops:
  0.0 3.6 %split.3 = (bf16[2,128,1536]{2,1,0:T(8,128)(2,1)}, bf16[2,128,1536]{2,1,0:T(8,128)(2,1)}) custom-call(bf16[1,256,2,4096]{3,2,1,0:T(2,128)(2,1)} %raw.3), custom_call_target="tpu_custom_call" | custom-call | bytes 4718592 | tf_op jit(solution)/shard_map/split/pallas_call | solution.py:140
  3.6 5.5 %collective-permute-start = (bf16[2,128,1536]{2,1,0:T(8,128)(2,1)}, bf16[2,128,1536]{2,1,0:T(8,128)(2,1)S(1)}, u32[]{:S(2)}, u32[]{:S(2)}) collective-permute-start(bf16[2,128,1536]{2,1,0:T(8,128)(2,1)} %get-tuple-element.56.second), channel_id=1, source_target_pairs={{0,16},{16,32},{32,48},{48,64},{64,80},{80,96},{96,112},{112,128},... | collective-permute-start | bytes 2359304 | tf_op jit(solution)/shard_map/ppermute | solution.py:380
  9.1 1.9 %collective-permute-start.1 = (bf16[2,128,1536]{2,1,0:T(8,128)(2,1)}, bf16[2,128,1536]{2,1,0:T(8,128)(2,1)S(1)}, u32[]{:S(2)}, u32[]{:S(2)}) collective-permute-start(bf16[2,128,1536]{2,1,0:T(8,128)(2,1)} %get-tuple-element.55.first), channel_id=1, source_target_pairs={{16,0},{32,16},{48,32},{64,48},{80,64},{96,80},{112,96},{128,112},... | collective-permute-start | bytes 2359304 | tf_op jit(solution)/shard_map/ppermute | solution.py:380
  11.0 5.0 %split.4 = (bf16[2,128,1536]{2,1,0:T(8,128)(2,1)}, bf16[2,128,1536]{2,1,0:T(8,128)(2,1)}, bf16[256,3072]{1,0:T(8,128)(2,1)}) custom-call(bf16[1,256,2,4096]{3,2,1,0:T(2,128)(2,1)} %raw.3), custom_call_target="tpu_custom_call" | custom-call | bytes 4718592 | tf_op jit(solution)/shard_map/split/pallas_call | solution.py:140
  16.0 5.1 %collective-permute-start.4 = (bf16[2,128,1536]{2,1,0:T(8,128)(2,1)}, bf16[2,128,1536]{2,1,0:T(8,128)(2,1)}, u32[]{:S(2)}, u32[]{:S(2)}) collective-permute-start(bf16[2,128,1536]{2,1,0:T(8,128)(2,1)} %get-tuple-element.49), channel_id=1, source_target_pairs={{0,16},{16,32},{32,48},{48,64},{64,80},{80,96},{96,112},{112,128},... | collective-permute-start | bytes 2359304 | tf_op jit(solution)/shard_map/ppermute | solution.py:380
  21.1 1.9 %collective-permute-start.5 = (bf16[2,128,1536]{2,1,0:T(8,128)(2,1)}, bf16[2,128,1536]{2,1,0:T(8,128)(2,1)}, u32[]{:S(2)}, u32[]{:S(2)}) collective-permute-start(bf16[2,128,1536]{2,1,0:T(8,128)(2,1)} %get-tuple-element.48), channel_id=1, source_target_pairs={{16,0},{32,16},{48,32},{64,48},{80,64},{96,80},{112,96},{128,112},... | collective-permute-start | bytes 2359304 | tf_op jit(solution)/shard_map/ppermute | solution.py:380
  23.1 0.5 fusion.2
  23.7 0.1 maximum_maximum_fusion.table_ref
  23.8 3.8 %split.5 = (bf16[2,128,1024]{2,1,0:T(8,128)(2,1)}, bf16[2,128,1024]{2,1,0:T(8,128)(2,1)}, bf16[256,2048]{1,0:T(8,128)(2,1)}) custom-call(bf16[1,256,2,4096]{3,2,1,0:T(2,128)(2,1)} %raw.3), custom_call_target="tpu_custom_call" | custom-call | bytes 3145728 | tf_op jit(solution)/shard_map/split/pallas_call | solution.py:140
  27.6 5.2 %collective-permute-done.1.right = bf16[2,128,1536]{2,1,0:T(8,128)(2,1)S(1)} collective-permute-done((bf16[2,128,1536]{2,1,0:T(8,128)(2,1)}, bf16[2,128,1536]{2,1,0:T(8,128)(2,1)S(1)}, u32[]{:S(2)}, u32[]{:S(2)}) %collective-permute-start.1) | collective-permute-done | bytes 786464 | tf_op jit(solution)/shard_map/ppermute | solution.py:380
  32.9 2.9 %white.1.white_ref = bf16[256,3072]{1,0:T(8,128)(2,1)S(1)} custom-call(bf16[2,128,1536]{2,1,0:T(8,128)(2,1)} %get-tuple-element.55.first, bf16[2,128,1536]{2,1,0:T(8,128)(2,1)} %get-tuple-element.56.second), custom_call_target="tpu_custom_call" | custom-call | bytes 3145728 | tf_op jit(solution)/shard_map/white/pallas_call | solution.py:154
  35.8 6.1 %early_pairs.2.refs_0_ = f32[1792,256]{1,0:T(8,128)} custom-call(bf16[2,128,1536]{2,1,0:T(8,128)(2,1)} %copy-done.3, bf16[2,128,1536]{2,1,0:T(8,128)(2,1)} %copy-done.4, f32[8,4096]{1,0:T(8,128)S(1)} %maximum_maximum_fusion.table_ref, bf16[256,3072]{1,0:T(8,128)(2,1)S(1)} %white.1.white_ref), custom_call_target="tpu_custom_call" | custom-call | flops 2818572288 | bytes 8388608 | tf_op jit(solution)/shard_map/early_pairs/pallas_call | solution.py:319
  41.9 2.2 %collective-permute-start.2 = (bf16[2,128,1024]{2,1,0:T(8,128)(2,1)}, bf16[2,128,1024]{2,1,0:T(8,128)(2,1)S(1)}, u32[]{:S(2)}, u32[]{:S(2)}) collective-permute-start(bf16[2,128,1024]{2,1,0:T(8,128)(2,1)} %get-tuple-element.57), channel_id=1, source_target_pairs={{0,16},{16,32},{32,48},{48,64},{64,80},{80,96},{96,112},{112,128},... | collective-permute-start | bytes 1572872 | tf_op jit(solution)/shard_map/ppermute | solution.py:380
  44.1 3.7 %collective-permute-start.3 = (bf16[2,128,1024]{2,1,0:T(8,128)(2,1)}, bf16[2,128,1024]{2,1,0:T(8,128)(2,1)}, u32[]{:S(2)}, u32[]{:S(2)}) collective-permute-start(bf16[2,128,1024]{2,1,0:T(8,128)(2,1)} %get-tuple-element.58), channel_id=1, source_target_pairs={{16,0},{32,16},{48,32},{64,48},{80,64},{96,80},{112,96},{128,112},... | collective-permute-start | bytes 1572872 | tf_op jit(solution)/shard_map/ppermute | solution.py:380
  48.4 0.7 copy.5.pairs
  49.1 0.6 bitcast_and_fusion.2
  50.3 0.1 conditional.1
  50.3 0.1 broadcast.71
  50.5 7.0 %early_pairs.3.before = f32[1792,256]{1,0:T(8,128)} custom-call(bf16[2,128,1536]{2,1,0:T(8,128)(2,1)} %collective-permute-done.4.left, bf16[2,128,1536]{2,1,0:T(8,128)(2,1)} %collective-permute-done.5.right, f32[8,4096]{1,0:T(8,128)S(1)} %maximum_maximum_fusion.table_ref, bf16[256,3072]{1,0:T(8,128)(2,1)} %get-tuple-element.60.white_ref, ...), custom_call_target="tpu_custom_call" | custom-call | flops 2818572288 | bytes 8388608 | tf_op jit(solution)/shard_map/early_pairs/pallas_call | solution.py:319
  57.5 2.1 %collective-permute-done.3.right = bf16[2,128,1024]{2,1,0:T(8,128)(2,1)} collective-permute-done((bf16[2,128,1024]{2,1,0:T(8,128)(2,1)}, bf16[2,128,1024]{2,1,0:T(8,128)(2,1)}, u32[]{:S(2)}, u32[]{:S(2)}) %collective-permute-start.3) | collective-permute-done | bytes 524320 | tf_op jit(solution)/shard_map/ppermute | solution.py:380
  59.6 6.3 %last_pairs.1 = (f32[8,240,128]{2,1,0:T(8,128)}, bf16[8,240,128]{2,1,0:T(8,128)(2,1)}) custom-call(s32[3,2]{1,0:T(4,128)} %copy.5.pairs, s32[1]{0:T(128)} %copy.8.count, bf16[2,128,1024]{2,1,0:T(8,128)(2,1)} %copy-done.5, bf16[2,128,1024]{2,1,0:T(8,128)(2,1)} %collective-permute-done.3.right, f32[8,4096]{1,0:T(8,128)S(1)} %maximum_maximum_fusion.table_ref, ...), custom_call_target="tpu_custom_call" | custom-call | flops 1879048192 | bytes 8388608 | tf_op jit(solution)/shard_map/last_pairs/pallas_call | solution.py:343
  65.9 2.1 %collective-permute-start.6 = (bf16[8,240,128]{2,1,0:T(8,128)(2,1)}, bf16[8,240,128]{2,1,0:T(8,128)(2,1)S(1)}, u32[]{:S(2)}, u32[]{:S(2)}) collective-permute-start(bf16[8,240,128]{2,1,0:T(8,128)(2,1)} %get-tuple-element.63), channel_id=1, source_target_pairs={{0,1},{1,0},{2,3},{3,2},{4,5},{5,4},{6,7},{7,6},{8,9},{9,8},{10,11... | collective-permute-start | bytes 1474568 | tf_op jit(solution)/shard_map/ppermute | solution.py:412
  68.0 2.0 %collective-permute-done.6 = bf16[8,240,128]{2,1,0:T(8,128)(2,1)S(1)} collective-permute-done((bf16[8,240,128]{2,1,0:T(8,128)(2,1)}, bf16[8,240,128]{2,1,0:T(8,128)(2,1)S(1)}, u32[]{:S(2)}, u32[]{:S(2)}) %collective-permute-start.6) | collective-permute-done | bytes 491552 | tf_op jit(solution)/shard_map/ppermute | solution.py:412
  70.0 1.0 add_convert_fusion.1
  71.1 1.9 %collective-permute-start.7 = (bf16[8,48,128]{2,1,0:T(8,128)(2,1)S(1)}, bf16[8,48,128]{2,1,0:T(8,128)(2,1)S(1)}, u32[]{:S(2)}, u32[]{:S(2)}) collective-permute-start(bf16[8,48,128]{2,1,0:T(8,128)(2,1)S(1)} %get-tuple-element.70), channel_id=1, source_target_pairs={{0,16},{16,0},{32,48},{48,32},{64,80},{80,64},{96,112},{112,96},{1... | collective-permute-start | bytes 294920 | tf_op jit(solution)/shard_map/ppermute | solution.py:422
  73.0 15.7 %collective-permute-start.8 = (bf16[8,48,128]{2,1,0:T(8,128)(2,1)S(1)}, bf16[8,48,128]{2,1,0:T(8,128)(2,1)S(1)}, u32[]{:S(2)}, u32[]{:S(2)}) collective-permute-start(bf16[8,48,128]{2,1,0:T(8,128)(2,1)S(1)} %get-tuple-element.71), channel_id=1, source_target_pairs={{16,32},{32,16},{48,64},{64,48},{80,96},{96,80},{112,128},{128,112... | collective-permute-start | bytes 294920 | tf_op jit(solution)/shard_map/ppermute | solution.py:423
  88.8 0.1 broadcast_in_dim.57
  89.0 0.1 broadcast_in_dim.54
  89.1 2.7 %collective-permute-done.8 = bf16[8,48,128]{2,1,0:T(8,128)(2,1)S(1)} collective-permute-done((bf16[8,48,128]{2,1,0:T(8,128)(2,1)S(1)}, bf16[8,48,128]{2,1,0:T(8,128)(2,1)S(1)}, u32[]{:S(2)}, u32[]{:S(2)}) %collective-permute-start.8) | collective-permute-done | bytes 98336 | tf_op jit(solution)/shard_map/ppermute | solution.py:423
  91.8 0.2 fusion
  92.0 19.3 %all_to_all.5 = bf16[8,144,128]{2,1,0:T(8,128)(2,1)S(1)} all-to-all(bf16[8,144,128]{2,1,0:T(8,128)(2,1)S(1)} %fusion), channel_id=1, replica_groups=mesh['sta'=32,'seg'=8,'band'=2] {'seg'}, dimensions={0} | all-to-all | bytes 589824 | tf_op jit(solution)/shard_map/all_to_all | solution.py:428
  111.3 0.6 broadcast_multiply_fusion
  (26 shorter events, 0.3 us)
Async XLA Ops:
  3.6 24.0 %collective-permute-start = (bf16[2,128,1536]{2,1,0:T(8,128)(2,1)}, bf16[2,128,1536]{2,1,0:T(8,128)(2,1)S(1)}, u32[]{:S(2)}, u32[]{:S(2)}) collective-permute-start(bf16[2,128,1536]{2,1,0:T(8,128)(2,1)} %get-tuple-element.56.second), channel_id=1, source_target_pairs={{0,16},{16,32},{32,48},{48,64},{64,80},{80,96},{96,112},{112,128},... | collective-permute-start | bytes 2359304 | tf_op jit(solution)/shard_map/ppermute | solution.py:380
  9.1 23.8 %collective-permute-start.1 = (bf16[2,128,1536]{2,1,0:T(8,128)(2,1)}, bf16[2,128,1536]{2,1,0:T(8,128)(2,1)S(1)}, u32[]{:S(2)}, u32[]{:S(2)}) collective-permute-start(bf16[2,128,1536]{2,1,0:T(8,128)(2,1)} %get-tuple-element.55.first), channel_id=1, source_target_pairs={{16,0},{32,16},{48,32},{64,48},{80,64},{96,80},{112,96},{128,112},... | collective-permute-start | bytes 2359304 | tf_op jit(solution)/shard_map/ppermute | solution.py:380
  16.0 34.4 %collective-permute-start.4 = (bf16[2,128,1536]{2,1,0:T(8,128)(2,1)}, bf16[2,128,1536]{2,1,0:T(8,128)(2,1)}, u32[]{:S(2)}, u32[]{:S(2)}) collective-permute-start(bf16[2,128,1536]{2,1,0:T(8,128)(2,1)} %get-tuple-element.49), channel_id=1, source_target_pairs={{0,16},{16,32},{32,48},{48,64},{64,80},{80,96},{96,112},{112,128},... | collective-permute-start | bytes 2359304 | tf_op jit(solution)/shard_map/ppermute | solution.py:380
  21.1 29.3 %collective-permute-start.5 = (bf16[2,128,1536]{2,1,0:T(8,128)(2,1)}, bf16[2,128,1536]{2,1,0:T(8,128)(2,1)}, u32[]{:S(2)}, u32[]{:S(2)}) collective-permute-start(bf16[2,128,1536]{2,1,0:T(8,128)(2,1)} %get-tuple-element.48), channel_id=1, source_target_pairs={{16,0},{32,16},{48,32},{64,48},{80,64},{96,80},{112,96},{128,112},... | collective-permute-start | bytes 2359304 | tf_op jit(solution)/shard_map/ppermute | solution.py:380
  27.6 8.1 %copy-start.3 = (bf16[2,128,1536]{2,1,0:T(8,128)(2,1)}, bf16[2,128,1536]{2,1,0:T(8,128)(2,1)S(1)}, u32[]{:S(2)}) copy-start(bf16[2,128,1536]{2,1,0:T(8,128)(2,1)S(1)} %collective-permute-done.left) | copy-start | bytes 2359300
  32.8 2.9 %copy-start.4 = (bf16[2,128,1536]{2,1,0:T(8,128)(2,1)}, bf16[2,128,1536]{2,1,0:T(8,128)(2,1)S(1)}, u32[]{:S(2)}) copy-start(bf16[2,128,1536]{2,1,0:T(8,128)(2,1)S(1)} %collective-permute-done.1.right) | copy-start | bytes 2359300
  35.8 12.6 %copy-start.1 = (s32[3,2]{0,1:T(2,128)S(1)}, s32[3,2]{0,1:T(2,128)}, u32[]{:S(2)}) copy-start(s32[3,2]{0,1:T(2,128)} %param.6) | copy-start | bytes 76
  41.9 15.6 %collective-permute-start.2 = (bf16[2,128,1024]{2,1,0:T(8,128)(2,1)}, bf16[2,128,1024]{2,1,0:T(8,128)(2,1)S(1)}, u32[]{:S(2)}, u32[]{:S(2)}) collective-permute-start(bf16[2,128,1024]{2,1,0:T(8,128)(2,1)} %get-tuple-element.57), channel_id=1, source_target_pairs={{0,16},{16,32},{32,48},{48,64},{64,80},{80,96},{96,112},{112,128},... | collective-permute-start | bytes 1572872 | tf_op jit(solution)/shard_map/ppermute | solution.py:380
  44.1 15.5 %collective-permute-start.3 = (bf16[2,128,1024]{2,1,0:T(8,128)(2,1)}, bf16[2,128,1024]{2,1,0:T(8,128)(2,1)}, u32[]{:S(2)}, u32[]{:S(2)}) collective-permute-start(bf16[2,128,1024]{2,1,0:T(8,128)(2,1)} %get-tuple-element.58), channel_id=1, source_target_pairs={{16,0},{32,16},{48,32},{64,48},{80,64},{96,80},{112,96},{128,112},... | collective-permute-start | bytes 1572872 | tf_op jit(solution)/shard_map/ppermute | solution.py:380
  50.4 9.2 %copy-start.2 = (bf16[256,2048]{1,0:T(8,128)(2,1)S(1)}, bf16[256,2048]{1,0:T(8,128)(2,1)}, u32[]{:S(2)}) copy-start(bf16[256,2048]{1,0:T(8,128)(2,1)} %get-tuple-element.59.white_ref) | copy-start | bytes 3145732
  57.5 2.1 %copy-start.5 = (bf16[2,128,1024]{2,1,0:T(8,128)(2,1)}, bf16[2,128,1024]{2,1,0:T(8,128)(2,1)S(1)}, u32[]{:S(2)}) copy-start(bf16[2,128,1024]{2,1,0:T(8,128)(2,1)S(1)} %collective-permute-done.2.left) | copy-start | bytes 1572868
  65.9 25.9 %copy-start = (f32[8,240,128]{2,1,0:T(8,128)S(1)}, f32[8,240,128]{2,1,0:T(8,128)}, u32[]{:S(2)}) copy-start(f32[8,240,128]{2,1,0:T(8,128)} %get-tuple-element.62) | copy-start | bytes 2949124
  65.9 4.1 %collective-permute-start.6 = (bf16[8,240,128]{2,1,0:T(8,128)(2,1)}, bf16[8,240,128]{2,1,0:T(8,128)(2,1)S(1)}, u32[]{:S(2)}, u32[]{:S(2)}) collective-permute-start(bf16[8,240,128]{2,1,0:T(8,128)(2,1)} %get-tuple-element.63), channel_id=1, source_target_pairs={{0,1},{1,0},{2,3},{3,2},{4,5},{5,4},{6,7},{7,6},{8,9},{9,8},{10,11... | collective-permute-start | bytes 1474568 | tf_op jit(solution)/shard_map/ppermute | solution.py:412
  71.1 18.0 %collective-permute-start.7 = (bf16[8,48,128]{2,1,0:T(8,128)(2,1)S(1)}, bf16[8,48,128]{2,1,0:T(8,128)(2,1)S(1)}, u32[]{:S(2)}, u32[]{:S(2)}) collective-permute-start(bf16[8,48,128]{2,1,0:T(8,128)(2,1)S(1)} %get-tuple-element.70), channel_id=1, source_target_pairs={{0,16},{16,0},{32,48},{48,32},{64,80},{80,64},{96,112},{112,96},{1... | collective-permute-start | bytes 294920 | tf_op jit(solution)/shard_map/ppermute | solution.py:422
  73.0 18.8 %collective-permute-start.8 = (bf16[8,48,128]{2,1,0:T(8,128)(2,1)S(1)}, bf16[8,48,128]{2,1,0:T(8,128)(2,1)S(1)}, u32[]{:S(2)}, u32[]{:S(2)}) collective-permute-start(bf16[8,48,128]{2,1,0:T(8,128)(2,1)S(1)} %get-tuple-element.71), channel_id=1, source_target_pairs={{16,32},{32,16},{48,64},{64,48},{80,96},{96,80},{112,128},{128,112... | collective-permute-start | bytes 294920 | tf_op jit(solution)/shard_map/ppermute | solution.py:423

commit v4 on v3

--- a/solution.py
+++ b/solution.py
@@ -96,12 +96,12 @@
     return pl.CostEstimate(flops=2 * SUMS[0] * SUMS[1] * 2 * bins, bytes_accessed=8 << 20, transcendentals=0)
 
 
-def slot_facts(pairs, count, slot):
+def slot_facts(slots, slot):
     first_block = lax.axis_index("sta") * 2
-    left, right = pairs[slot, 0] - first_block, pairs[slot, 1] - first_block
+    left, right = slots[2 * slot] - first_block, slots[2 * slot + 1] - first_block
     kind = jnp.where(right == -1, FROM_LEFT, jnp.where(right == 2, FROM_RIGHT, LOCAL))
     kind = jnp.where((right == -2) | (right == 3), REMOTE, kind)
-    return jnp.where(slot < count[0], kind, DEAD), left, right
+    return jnp.where(slot < slots[2 * PAIR_CAP], kind, DEAD), left, right
 
 
 def put_white(planes, white):
@@ -170,12 +170,12 @@
     return starts
 
 
-def local_kernel(starts, pairs, count, *refs):
+def local_kernel(starts, slots, *refs):
     chunks = len(starts) - 1
     whites, (table_ref, local_ref, white, parts_first, parts_second, sums) = refs[:chunks], refs[chunks:]
     step = pl.program_id(0)
     last = pl.num_programs(0) - 1
-    facts = [slot_facts(pairs, count, slot) for slot in range(PAIR_CAP)]
+    facts = [slot_facts(slots, slot) for slot in range(PAIR_CAP)]
     here = [kind == LOCAL for kind, _, _ in facts]
 
     @pl.when(step == 0)
@@ -190,10 +190,13 @@
 
     table = table_ref[...]
     for block, parts in enumerate((parts_first, parts_second)):
-        rows = white.at[block * STA : (block + 1) * STA, :]
-        put_parts(parts, rows[:, :STEP], rows[:, STEP:], table)
-    sums[:SUM_ROWS, :] += product(parts_first[...], white[...])
-    sums[SUM_ROWS:, :] += product(parts_second[...], white[...])
+        mine = [here[slot] & (facts[slot][1] == block) for slot in range(PAIR_CAP)]
+
+        @pl.when(mine[0] | mine[1] | mine[2])
+        def _():
+            rows = white.at[block * STA : (block + 1) * STA, :]
+            put_parts(parts, rows[:, :STEP], rows[:, STEP:], table)
+            sums[block * SUM_ROWS : (block + 1) * SUM_ROWS, :] += product(parts[...], white[...])
 
     @pl.when(step == last)
     def _():
@@ -210,7 +213,7 @@
                 local_ref[slot] = jnp.zeros((TILE, STA), jnp.float32)
 
 
-def local_part(pair_list, pair_count, whites, table):
+def local_part(slots, whites, table):
     bins = table.shape[1]
     starts = chunk_starts([white.shape[1] // 2 for white in whites])
 
@@ -224,7 +227,7 @@
         functools.partial(local_kernel, tuple(starts)),
         out_shape=jax.ShapeDtypeStruct((PAIR_CAP, TILE, STA), jnp.float32),
         grid_spec=pltpu.PrefetchScalarGridSpec(
-            num_scalar_prefetch=2,
+            num_scalar_prefetch=1,
             grid=(starts[-1],),
             in_specs=specs + [pl.BlockSpec((8, STEP), lambda i, *_: (0, i))],
             out_specs=whole((PAIR_CAP, TILE, STA)),
@@ -233,7 +236,7 @@
         compiler_params=params(),
         cost_estimate=cost(bins // 4),
         name="local_pairs",
-    )(pair_list, pair_count, *whites, table)
+    )(slots, *whites, table)
 
 
 def scratch():
@@ -259,7 +262,7 @@
 
 
 def last_kernel(
-    pairs, count, left, right, table_ref, white_ref, before, local, keep_ref, send_ref,
+    slots, left, right, table_ref, white_ref, before, local, keep_ref, send_ref,
     parts_left, parts_right, sums, before_here, local_ref, arrived,
 ):
     step = pl.program_id(0)
@@ -292,7 +295,7 @@
             send_ref[:, rows, :] = jnp.where(even_core, odd, even).astype(jnp.bfloat16)
 
         for slot in range(PAIR_CAP):
-            kind, column_block, _ = slot_facts(pairs, count, slot)
+            kind, column_block, _ = slot_facts(slots, slot)
 
             @pl.when(kind < LOCAL)
             def _():
@@ -335,7 +338,7 @@
     )(left, right, table, white, *before)
 
 
-def last_part(pair_list, pair_count, left, right, white, table, before, local):
+def last_part(slots, left, right, white, table, before, local):
     bins = left.shape[2]
     base = (table.shape[1] - bins) // STEP
     result = (8, OUT_ROWS, STA)
@@ -344,7 +347,7 @@
         last_kernel,
         out_shape=(jax.ShapeDtypeStruct(result, jnp.float32), jax.ShapeDtypeStruct(result, jnp.bfloat16)),
         grid_spec=pltpu.PrefetchScalarGridSpec(
-            num_scalar_prefetch=2,
+            num_scalar_prefetch=1,
             grid=(bins // STEP,),
             in_specs=[
                 plane_spec(),
@@ -365,7 +368,7 @@
         compiler_params=params(),
         cost_estimate=cost(bins),
         name="last_pairs",
-    )(pair_list, pair_count, left, right, table, white, before, local)
+    )(slots, left, right, table, white, before, local)
 
 
 def body(raw_spectra, pair_list, pair_count):
@@ -378,6 +381,11 @@
 
     def send(pair):
         return lax.ppermute(pair[1], "sta", to_right), lax.ppermute(pair[0], "sta", to_left)
+
+    right_id = pair_list[:, 1] - position * 2
+    live = jnp.arange(PAIR_CAP) < pair_count[0]
+    any_local = jnp.any(live & (right_id >= 0) & (right_id <= 1))
+    slots = jnp.concatenate([pair_list.reshape(-1), pair_count])
 
     planes = []
     received = []
@@ -396,18 +404,16 @@
     before = early_part(*received[0], whites[0], table, 0)
     ending, before = lax.optimization_barrier((planes[-1][:2], before))
     received.append(send(ending))
-    right_id = pair_list[:, 1] - position * 2
-    live = jnp.arange(PAIR_CAP) < pair_count[0]
     local = lax.cond(
-        jnp.any(live & (right_id >= 0) & (right_id <= 1)),
-        lambda: local_part(pair_list, pair_count, whites, table),
+        any_local,
+        lambda: local_part(slots, whites, table),
         lambda: jnp.zeros((PAIR_CAP, TILE, STA), jnp.float32),
     )
     start = CHUNKS[0]
     for count, pair, white in zip(CHUNKS[1:-1], received[1:-1], whites[1:-1]):
         before = early_part(*pair, white, table, start, before)
         start += count
-    keep, send_half = last_part(pair_list, pair_count, *received[-1], whites[-1], table, before, local)
+    keep, send_half = last_part(slots, *received[-1], whites[-1], table, before, local)
 
     other = lax.ppermute(send_half, "band", [(0, 1), (1, 0)])
     own_rows = PAIR_CAP * LAGS * 8

time: 113 us -> 106 us (0.938)
  the two profiles are of different devices: /device:TPU:196 before, /device:TPU:6 now
where the time goes in v4:
time: 106 us
  starting transfers between devices  39.6 us (37%)
  Pallas kernels  34.7 us (33%)
  blocking collectives  19.3 us (18%)
  waiting for transfers between devices  6.55 us (6%)
  other arithmetic  3.3 us (3%)
  between operations  1.53 us (1%)
    ppermute x3, starting transfers between devices, send(): lax.ppermute(pair[0], 'sta', to_left)  21 us
    all_to_all x1, blocking collectives, body(): gathered = lax.all_to_all(pieces.reshape(8, own_rows, STA), 'seg', 0, 0)  19.3 us
    pallas_call x2, Pallas kernels, early_part(): pl.pallas_call(early_kernel, out_shape=jax.ShapeDtypeStruct(SUMS, jnp.flo...  13.1 us
    pallas_call x3, Pallas kernels, split(): pl.pallas_call(split_kernel, out_shape=(shape, shape) + (white_shape(coun...  12.4 us
    ppermute x3, starting transfers between devices, send(): lax.ppermute(pair[1], 'sta', to_right)  8.09 us
    ppermute x1, starting transfers between devices, body(): got_odd = lax.ppermute(foreign[:, LAGS * 8:], 'sta', swap_odd)  6.5 us
    pallas_call x1, Pallas kernels, last_part(): pl.pallas_call(last_kernel, out_shape=(jax.ShapeDtypeStruct(result, jnp.f...  6.15 us
    pallas_call x1, Pallas kernels, white_part(): pl.pallas_call(white_kernel, out_shape=white_shape(count), grid=(count //...  3.02 us
  transfers between devices with their start and end apart: 9, of which 4 were waited for; matrix products, arithmetic and copies ran while one was open for 2% of the time, Pallas kernels for 24%

profile of v4, /device:TPU:6, one launch (start us, length us, event | category | flops | bytes accessed | tf_op | source)
XLA Modules:
  0.0 105.6 jit_solution(13088005692792276302)
XLA Ops:
  0.0 3.6 %split.3 = (bf16[2,128,1536]{2,1,0:T(8,128)(2,1)}, bf16[2,128,1536]{2,1,0:T(8,128)(2,1)}) custom-call(bf16[1,256,2,4096]{3,2,1,0:T(2,128)(2,1)} %raw.3), custom_call_target="tpu_custom_call" | custom-call | bytes 4718592 | tf_op jit(solution)/shard_map/split/pallas_call | solution.py:140
  3.6 4.3 %collective-permute-start = (bf16[2,128,1536]{2,1,0:T(8,128)(2,1)}, bf16[2,128,1536]{2,1,0:T(8,128)(2,1)S(1)}, u32[]{:S(2)}, u32[]{:S(2)}) collective-permute-start(bf16[2,128,1536]{2,1,0:T(8,128)(2,1)} %get-tuple-element.53.second), channel_id=1, source_target_pairs={{0,16},{16,32},{32,48},{48,64},{64,80},{80,96},{96,112},{112,128},... | collective-permute-start | bytes 2359304 | tf_op jit(solution)/shard_map/ppermute | solution.py:383
  7.9 8.9 %collective-permute-start.1 = (bf16[2,128,1536]{2,1,0:T(8,128)(2,1)}, bf16[2,128,1536]{2,1,0:T(8,128)(2,1)S(1)}, u32[]{:S(2)}, u32[]{:S(2)}) collective-permute-start(bf16[2,128,1536]{2,1,0:T(8,128)(2,1)} %get-tuple-element.52.first), channel_id=1, source_target_pairs={{16,0},{32,16},{48,32},{64,48},{80,64},{96,80},{112,96},{128,112},... | collective-permute-start | bytes 2359304 | tf_op jit(solution)/shard_map/ppermute | solution.py:383
  16.7 5.0 %split.4 = (bf16[2,128,1536]{2,1,0:T(8,128)(2,1)}, bf16[2,128,1536]{2,1,0:T(8,128)(2,1)}, bf16[256,3072]{1,0:T(8,128)(2,1)}) custom-call(bf16[1,256,2,4096]{3,2,1,0:T(2,128)(2,1)} %raw.3), custom_call_target="tpu_custom_call" | custom-call | bytes 4718592 | tf_op jit(solution)/shard_map/split/pallas_call | solution.py:140
  21.7 1.9 %collective-permute-start.4 = (bf16[2,128,1536]{2,1,0:T(8,128)(2,1)}, bf16[2,128,1536]{2,1,0:T(8,128)(2,1)}, u32[]{:S(2)}, u32[]{:S(2)}) collective-permute-start(bf16[2,128,1536]{2,1,0:T(8,128)(2,1)} %get-tuple-element.46), channel_id=1, source_target_pairs={{0,16},{16,32},{32,48},{48,64},{64,80},{80,96},{96,112},{112,128},... | collective-permute-start | bytes 2359304 | tf_op jit(solution)/shard_map/ppermute | solution.py:383
  23.7 6.0 %collective-permute-start.5 = (bf16[2,128,1536]{2,1,0:T(8,128)(2,1)}, bf16[2,128,1536]{2,1,0:T(8,128)(2,1)}, u32[]{:S(2)}, u32[]{:S(2)}) collective-permute-start(bf16[2,128,1536]{2,1,0:T(8,128)(2,1)} %get-tuple-element.45), channel_id=1, source_target_pairs={{16,0},{32,16},{48,32},{64,48},{80,64},{96,80},{112,96},{128,112},... | collective-permute-start | bytes 2359304 | tf_op jit(solution)/shard_map/ppermute | solution.py:383
  29.7 0.5 fusion.2
  30.4 0.1 maximum_maximum_fusion.table_ref
  30.5 3.8 %split.5 = (bf16[2,128,1024]{2,1,0:T(8,128)(2,1)}, bf16[2,128,1024]{2,1,0:T(8,128)(2,1)}, bf16[256,2048]{1,0:T(8,128)(2,1)}) custom-call(bf16[1,256,2,4096]{3,2,1,0:T(2,128)(2,1)} %raw.3), custom_call_target="tpu_custom_call" | custom-call | bytes 3145728 | tf_op jit(solution)/shard_map/split/pallas_call | solution.py:140
  34.9 0.1 copy.5
  35.0 0.1 reshape.56
  35.1 3.0 %white.1.white_ref = bf16[256,3072]{1,0:T(8,128)(2,1)S(1)} custom-call(bf16[2,128,1536]{2,1,0:T(8,128)(2,1)} %get-tuple-element.52.first, bf16[2,128,1536]{2,1,0:T(8,128)(2,1)} %get-tuple-element.53.second), custom_call_target="tpu_custom_call" | custom-call | bytes 3145728 | tf_op jit(solution)/shard_map/white/pallas_call | solution.py:154
  38.1 6.1 %early_pairs.2.refs_0_ = f32[1792,256]{1,0:T(8,128)} custom-call(bf16[2,128,1536]{2,1,0:T(8,128)(2,1)} %copy-done.3, bf16[2,128,1536]{2,1,0:T(8,128)(2,1)} %copy-done.4, f32[8,4096]{1,0:T(8,128)S(1)} %maximum_maximum_fusion.table_ref, bf16[256,3072]{1,0:T(8,128)(2,1)S(1)} %white.1.white_ref), custom_call_target="tpu_custom_call" | custom-call | flops 2818572288 | bytes 8388608 | tf_op jit(solution)/shard_map/early_pairs/pallas_call | solution.py:322
  44.2 1.9 %collective-permute-start.2 = (bf16[2,128,1024]{2,1,0:T(8,128)(2,1)}, bf16[2,128,1024]{2,1,0:T(8,128)(2,1)S(1)}, u32[]{:S(2)}, u32[]{:S(2)}) collective-permute-start(bf16[2,128,1024]{2,1,0:T(8,128)(2,1)} %get-tuple-element.54), channel_id=1, source_target_pairs={{0,16},{16,32},{32,48},{48,64},{64,80},{80,96},{96,112},{112,128},... | collective-permute-start | bytes 1572872 | tf_op jit(solution)/shard_map/ppermute | solution.py:383
  46.2 6.1 %collective-permute-start.3 = (bf16[2,128,1024]{2,1,0:T(8,128)(2,1)}, bf16[2,128,1024]{2,1,0:T(8,128)(2,1)}, u32[]{:S(2)}, u32[]{:S(2)}) collective-permute-start(bf16[2,128,1024]{2,1,0:T(8,128)(2,1)} %get-tuple-element.55), channel_id=1, source_target_pairs={{16,0},{32,16},{48,32},{64,48},{80,64},{96,80},{112,96},{128,112},... | collective-permute-start | bytes 1572872 | tf_op jit(solution)/shard_map/ppermute | solution.py:383
  52.3 0.6 bitcast_and_fusion.2
  53.6 0.1 conditional.1
  53.8 7.0 %early_pairs.3.before = f32[1792,256]{1,0:T(8,128)} custom-call(bf16[2,128,1536]{2,1,0:T(8,128)(2,1)} %collective-permute-done.4.left, bf16[2,128,1536]{2,1,0:T(8,128)(2,1)} %collective-permute-done.5.right, f32[8,4096]{1,0:T(8,128)S(1)} %maximum_maximum_fusion.table_ref, bf16[256,3072]{1,0:T(8,128)(2,1)} %get-tuple-element.57.white_ref, ...), custom_call_target="tpu_custom_call" | custom-call | flops 2818572288 | bytes 8388608 | tf_op jit(solution)/shard_map/early_pairs/pallas_call | solution.py:322
  60.8 0.5 collective-permute-done.2.left
  61.3 1.3 %collective-permute-done.3.right = bf16[2,128,1024]{2,1,0:T(8,128)(2,1)} collective-permute-done((bf16[2,128,1024]{2,1,0:T(8,128)(2,1)}, bf16[2,128,1024]{2,1,0:T(8,128)(2,1)}, u32[]{:S(2)}, u32[]{:S(2)}) %collective-permute-start.3) | collective-permute-done | bytes 524320 | tf_op jit(solution)/shard_map/ppermute | solution.py:383
  62.6 6.1 %last_pairs.1 = (f32[8,240,128]{2,1,0:T(8,128)}, bf16[8,240,128]{2,1,0:T(8,128)(2,1)}) custom-call(s32[7]{0:T(128)S(1)} %pad_add_fusion.slots, bf16[2,128,1024]{2,1,0:T(8,128)(2,1)} %copy-done.5, bf16[2,128,1024]{2,1,0:T(8,128)(2,1)} %collective-permute-done.3.right, f32[8,4096]{1,0:T(8,128)S(1)} %maximum_maximum_fusion.table_ref, ...), custom_call_target="tpu_custom_call" | custom-call | flops 1879048192 | bytes 8388608 | tf_op jit(solution)/shard_map/last_pairs/pallas_call | solution.py:346
  68.7 2.1 %collective-permute-start.6 = (bf16[8,240,128]{2,1,0:T(8,128)(2,1)}, bf16[8,240,128]{2,1,0:T(8,128)(2,1)S(1)}, u32[]{:S(2)}, u32[]{:S(2)}) collective-permute-start(bf16[8,240,128]{2,1,0:T(8,128)(2,1)} %get-tuple-element.60), channel_id=1, source_target_pairs={{0,1},{1,0},{2,3},{3,2},{4,5},{5,4},{6,7},{7,6},{8,9},{9,8},{10,11... | collective-permute-start | bytes 1474568 | tf_op jit(solution)/shard_map/ppermute | solution.py:418
  70.8 2.0 %collective-permute-done.6 = bf16[8,240,128]{2,1,0:T(8,128)(2,1)S(1)} collective-permute-done((bf16[8,240,128]{2,1,0:T(8,128)(2,1)}, bf16[8,240,128]{2,1,0:T(8,128)(2,1)S(1)}, u32[]{:S(2)}, u32[]{:S(2)}) %collective-permute-start.6) | collective-permute-done | bytes 491552 | tf_op jit(solution)/shard_map/ppermute | solution.py:418
  72.8 1.0 add_convert_fusion.1
  73.9 1.9 %collective-permute-start.7 = (bf16[8,48,128]{2,1,0:T(8,128)(2,1)S(1)}, bf16[8,48,128]{2,1,0:T(8,128)(2,1)S(1)}, u32[]{:S(2)}, u32[]{:S(2)}) collective-permute-start(bf16[8,48,128]{2,1,0:T(8,128)(2,1)S(1)} %get-tuple-element.61), channel_id=1, source_target_pairs={{0,16},{16,0},{32,48},{48,32},{64,80},{80,64},{96,112},{112,96},{1... | collective-permute-start | bytes 294920 | tf_op jit(solution)/shard_map/ppermute | solution.py:428
  75.8 6.5 %collective-permute-start.8 = (bf16[8,48,128]{2,1,0:T(8,128)(2,1)S(1)}, bf16[8,48,128]{2,1,0:T(8,128)(2,1)S(1)}, u32[]{:S(2)}, u32[]{:S(2)}) collective-permute-start(bf16[8,48,128]{2,1,0:T(8,128)(2,1)S(1)} %get-tuple-element.62), channel_id=1, source_target_pairs={{16,32},{32,16},{48,64},{64,48},{80,96},{96,80},{112,128},{128,112... | collective-permute-start | bytes 294920 | tf_op jit(solution)/shard_map/ppermute | solution.py:429
  82.4 0.1 broadcast_in_dim.57
  82.6 0.1 broadcast_in_dim.54
  82.7 2.7 %collective-permute-done.8 = bf16[8,48,128]{2,1,0:T(8,128)(2,1)S(1)} collective-permute-done((bf16[8,48,128]{2,1,0:T(8,128)(2,1)S(1)}, bf16[8,48,128]{2,1,0:T(8,128)(2,1)S(1)}, u32[]{:S(2)}, u32[]{:S(2)}) %collective-permute-start.8) | collective-permute-done | bytes 98336 | tf_op jit(solution)/shard_map/ppermute | solution.py:429
  85.4 0.2 fusion
  85.6 19.3 %all_to_all.5 = bf16[8,144,128]{2,1,0:T(8,128)(2,1)S(1)} all-to-all(bf16[8,144,128]{2,1,0:T(8,128)(2,1)S(1)} %fusion), channel_id=1, replica_groups=mesh['sta'=32,'seg'=8,'band'=2] {'seg'}, dimensions={0} | all-to-all | bytes 589824 | tf_op jit(solution)/shard_map/all_to_all | solution.py:434
  104.9 0.6 broadcast_multiply_fusion
  (28 shorter events, 0.5 us)
Async XLA Ops:
  3.6 31.5 %collective-permute-start = (bf16[2,128,1536]{2,1,0:T(8,128)(2,1)}, bf16[2,128,1536]{2,1,0:T(8,128)(2,1)S(1)}, u32[]{:S(2)}, u32[]{:S(2)}) collective-permute-start(bf16[2,128,1536]{2,1,0:T(8,128)(2,1)} %get-tuple-element.53.second), channel_id=1, source_target_pairs={{0,16},{16,32},{32,48},{48,64},{64,80},{80,96},{96,112},{112,128},... | collective-permute-start | bytes 2359304 | tf_op jit(solution)/shard_map/ppermute | solution.py:383
  7.9 27.2 %collective-permute-start.1 = (bf16[2,128,1536]{2,1,0:T(8,128)(2,1)}, bf16[2,128,1536]{2,1,0:T(8,128)(2,1)S(1)}, u32[]{:S(2)}, u32[]{:S(2)}) collective-permute-start(bf16[2,128,1536]{2,1,0:T(8,128)(2,1)} %get-tuple-element.52.first), channel_id=1, source_target_pairs={{16,0},{32,16},{48,32},{64,48},{80,64},{96,80},{112,96},{128,112},... | collective-permute-start | bytes 2359304 | tf_op jit(solution)/shard_map/ppermute | solution.py:383
  21.7 32.0 %collective-permute-start.4 = (bf16[2,128,1536]{2,1,0:T(8,128)(2,1)}, bf16[2,128,1536]{2,1,0:T(8,128)(2,1)}, u32[]{:S(2)}, u32[]{:S(2)}) collective-permute-start(bf16[2,128,1536]{2,1,0:T(8,128)(2,1)} %get-tuple-element.46), channel_id=1, source_target_pairs={{0,16},{16,32},{32,48},{48,64},{64,80},{80,96},{96,112},{112,128},... | collective-permute-start | bytes 2359304 | tf_op jit(solution)/shard_map/ppermute | solution.py:383
  23.7 30.1 %collective-permute-start.5 = (bf16[2,128,1536]{2,1,0:T(8,128)(2,1)}, bf16[2,128,1536]{2,1,0:T(8,128)(2,1)}, u32[]{:S(2)}, u32[]{:S(2)}) collective-permute-start(bf16[2,128,1536]{2,1,0:T(8,128)(2,1)} %get-tuple-element.45), channel_id=1, source_target_pairs={{16,0},{32,16},{48,32},{64,48},{80,64},{96,80},{112,96},{128,112},... | collective-permute-start | bytes 2359304 | tf_op jit(solution)/shard_map/ppermute | solution.py:383
  30.4 4.4 %copy-start.1 = (s32[3,2]{0,1:T(2,128)S(1)}, s32[3,2]{0,1:T(2,128)}, u32[]{:S(2)}) copy-start(s32[3,2]{0,1:T(2,128)} %param.6) | copy-start | bytes 76
  35.1 3.0 %copy-start.3 = (bf16[2,128,1536]{2,1,0:T(8,128)(2,1)}, bf16[2,128,1536]{2,1,0:T(8,128)(2,1)S(1)}, u32[]{:S(2)}) copy-start(bf16[2,128,1536]{2,1,0:T(8,128)(2,1)S(1)} %collective-permute-done.left) | copy-start | bytes 2359300
  35.1 3.1 %copy-start.4 = (bf16[2,128,1536]{2,1,0:T(8,128)(2,1)}, bf16[2,128,1536]{2,1,0:T(8,128)(2,1)S(1)}, u32[]{:S(2)}) copy-start(bf16[2,128,1536]{2,1,0:T(8,128)(2,1)S(1)} %collective-permute-done.1.right) | copy-start | bytes 2359300
  44.2 17.0 %collective-permute-start.2 = (bf16[2,128,1024]{2,1,0:T(8,128)(2,1)}, bf16[2,128,1024]{2,1,0:T(8,128)(2,1)S(1)}, u32[]{:S(2)}, u32[]{:S(2)}) collective-permute-start(bf16[2,128,1024]{2,1,0:T(8,128)(2,1)} %get-tuple-element.54), channel_id=1, source_target_pairs={{0,16},{16,32},{32,48},{48,64},{64,80},{80,96},{96,112},{112,128},... | collective-permute-start | bytes 1572872 | tf_op jit(solution)/shard_map/ppermute | solution.py:383
  46.2 16.4 %collective-permute-start.3 = (bf16[2,128,1024]{2,1,0:T(8,128)(2,1)}, bf16[2,128,1024]{2,1,0:T(8,128)(2,1)}, u32[]{:S(2)}, u32[]{:S(2)}) collective-permute-start(bf16[2,128,1024]{2,1,0:T(8,128)(2,1)} %get-tuple-element.55), channel_id=1, source_target_pairs={{16,0},{32,16},{48,32},{64,48},{80,64},{96,80},{112,96},{128,112},... | collective-permute-start | bytes 1572872 | tf_op jit(solution)/shard_map/ppermute | solution.py:383
  53.7 8.8 %copy-start.2 = (bf16[256,2048]{1,0:T(8,128)(2,1)S(1)}, bf16[256,2048]{1,0:T(8,128)(2,1)}, u32[]{:S(2)}) copy-start(bf16[256,2048]{1,0:T(8,128)(2,1)} %get-tuple-element.56.white_ref) | copy-start | bytes 3145732
  61.3 1.3 %copy-start.5 = (bf16[2,128,1024]{2,1,0:T(8,128)(2,1)}, bf16[2,128,1024]{2,1,0:T(8,128)(2,1)S(1)}, u32[]{:S(2)}) copy-start(bf16[2,128,1024]{2,1,0:T(8,128)(2,1)S(1)} %collective-permute-done.2.left) | copy-start | bytes 1572868
  68.7 16.7 %copy-start = (f32[8,240,128]{2,1,0:T(8,128)S(1)}, f32[8,240,128]{2,1,0:T(8,128)}, u32[]{:S(2)}) copy-start(f32[8,240,128]{2,1,0:T(8,128)} %get-tuple-element.59) | copy-start | bytes 2949124
  68.7 4.1 %collective-permute-start.6 = (bf16[8,240,128]{2,1,0:T(8,128)(2,1)}, bf16[8,240,128]{2,1,0:T(8,128)(2,1)S(1)}, u32[]{:S(2)}, u32[]{:S(2)}) collective-permute-start(bf16[8,240,128]{2,1,0:T(8,128)(2,1)} %get-tuple-element.60), channel_id=1, source_target_pairs={{0,1},{1,0},{2,3},{3,2},{4,5},{5,4},{6,7},{7,6},{8,9},{9,8},{10,11... | collective-permute-start | bytes 1474568 | tf_op jit(solution)/shard_map/ppermute | solution.py:418
  73.9 8.8 %collective-permute-start.7 = (bf16[8,48,128]{2,1,0:T(8,128)(2,1)S(1)}, bf16[8,48,128]{2,1,0:T(8,128)(2,1)S(1)}, u32[]{:S(2)}, u32[]{:S(2)}) collective-permute-start(bf16[8,48,128]{2,1,0:T(8,128)(2,1)S(1)} %get-tuple-element.61), channel_id=1, source_target_pairs={{0,16},{16,0},{32,48},{48,32},{64,80},{80,64},{96,112},{112,96},{1... | collective-permute-start | bytes 294920 | tf_op jit(solution)/shard_map/ppermute | solution.py:428
  75.8 9.6 %collective-permute-start.8 = (bf16[8,48,128]{2,1,0:T(8,128)(2,1)S(1)}, bf16[8,48,128]{2,1,0:T(8,128)(2,1)S(1)}, u32[]{:S(2)}, u32[]{:S(2)}) collective-permute-start(bf16[8,48,128]{2,1,0:T(8,128)(2,1)S(1)} %get-tuple-element.62), channel_id=1, source_target_pairs={{16,32},{32,16},{48,64},{64,48},{80,96},{96,80},{112,128},{128,112... | collective-permute-start | bytes 294920 | tf_op jit(solution)/shard_map/ppermute | solution.py:429

commit v5 on v4

--- a/solution.py
+++ b/solution.py
@@ -15,6 +15,7 @@
 PAIR_CAP = 3
 TURNS = 3
 STEP = 512
+PLAIN_STEP = 768
 EPSILON = 1e-06
 FROM_LEFT, FROM_RIGHT, LOCAL, REMOTE, DEAD = 0, 1, 2, 3, 4
 CHUNKS = (1536, 1536, 1024)
@@ -137,12 +138,14 @@
 
 def split(raw_spectra, start, count, with_white):
     shape = jax.ShapeDtypeStruct((2, STA, count), jnp.bfloat16)
+    step = STEP if with_white else PLAIN_STEP
+    plane = pl.BlockSpec((2, STA, step), lambda i: (0, 0, i))
     return pl.pallas_call(
         split_kernel,
         out_shape=(shape, shape) + (white_shape(count),) * with_white,
-        grid=(count // STEP,),
-        in_specs=[pl.BlockSpec((1, 2 * STA, 2, STEP), lambda i: (0, 0, 0, start // STEP + i))],
-        out_specs=(plane_spec(), plane_spec()) + (white_spec(),) * with_white,
+        grid=(count // step,),
+        in_specs=[pl.BlockSpec((1, 2 * STA, 2, step), lambda i: (0, 0, 0, start // step + i))],
+        out_specs=(plane, plane) + (white_spec(),) * with_white,
         compiler_params=params(),
         cost_estimate=pl.CostEstimate(flops=0, bytes_accessed=24 * STA * count, transcendentals=0),
         name="split",

time: 106 us -> 105 us (level)
  no operation moved by 1% of the time
where the time goes in v5:
time: 105 us
  starting transfers between devices  39.6 us (38%)
  Pallas kernels  33.7 us (32%)
  blocking collectives  19.3 us (18%)
  waiting for transfers between devices  6.55 us (6%)
  other arithmetic  3.3 us (3%)
  between operations  1.53 us (1%)
    ppermute x3, starting transfers between devices, send(): lax.ppermute(pair[0], 'sta', to_left)  21 us
    all_to_all x1, blocking collectives, body(): gathered = lax.all_to_all(pieces.reshape(8, own_rows, STA), 'seg', 0, 0)  19.3 us
    pallas_call x2, Pallas kernels, early_part(): pl.pallas_call(early_kernel, out_shape=jax.ShapeDtypeStruct(SUMS, jnp.flo...  13.1 us
    pallas_call x3, Pallas kernels, split(): pl.pallas_call(split_kernel, out_shape=(shape, shape) + (white_shape(coun...  11.4 us
    ppermute x3, starting transfers between devices, send(): lax.ppermute(pair[1], 'sta', to_right)  8.09 us
    ppermute x1, starting transfers between devices, body(): got_odd = lax.ppermute(foreign[:, LAGS * 8:], 'sta', swap_odd)  6.5 us
    pallas_call x1, Pallas kernels, last_part(): pl.pallas_call(last_kernel, out_shape=(jax.ShapeDtypeStruct(result, jnp.f...  6.15 us
    pallas_call x1, Pallas kernels, white_part(): pl.pallas_call(white_kernel, out_shape=white_shape(count), grid=(count //...  3.02 us
  transfers between devices with their start and end apart: 9, of which 4 were waited for; matrix products, arithmetic and copies ran while one was open for 2% of the time, Pallas kernels for 24%

profile of v5, /device:TPU:6, one launch (start us, length us, event | category | flops | bytes accessed | tf_op | source)
XLA Modules:
  0.0 104.6 jit_solution(5388065513093551535)
XLA Ops:
  0.0 2.6 %split.3 = (bf16[2,128,1536]{2,1,0:T(8,128)(2,1)}, bf16[2,128,1536]{2,1,0:T(8,128)(2,1)}) custom-call(bf16[1,256,2,4096]{3,2,1,0:T(2,128)(2,1)} %raw.3), custom_call_target="tpu_custom_call" | custom-call | bytes 4718592 | tf_op jit(solution)/shard_map/split/pallas_call | solution.py:143
  2.6 4.3 %collective-permute-start = (bf16[2,128,1536]{2,1,0:T(8,128)(2,1)}, bf16[2,128,1536]{2,1,0:T(8,128)(2,1)S(1)}, u32[]{:S(2)}, u32[]{:S(2)}) collective-permute-start(bf16[2,128,1536]{2,1,0:T(8,128)(2,1)} %get-tuple-element.53.second), channel_id=1, source_target_pairs={{0,16},{16,32},{32,48},{48,64},{64,80},{80,96},{96,112},{112,128},... | collective-permute-start | bytes 2359304 | tf_op jit(solution)/shard_map/ppermute | solution.py:386
  6.9 8.9 %collective-permute-start.1 = (bf16[2,128,1536]{2,1,0:T(8,128)(2,1)}, bf16[2,128,1536]{2,1,0:T(8,128)(2,1)S(1)}, u32[]{:S(2)}, u32[]{:S(2)}) collective-permute-start(bf16[2,128,1536]{2,1,0:T(8,128)(2,1)} %get-tuple-element.52.first), channel_id=1, source_target_pairs={{16,0},{32,16},{48,32},{64,48},{80,64},{96,80},{112,96},{128,112},... | collective-permute-start | bytes 2359304 | tf_op jit(solution)/shard_map/ppermute | solution.py:386
  15.8 5.0 %split.4 = (bf16[2,128,1536]{2,1,0:T(8,128)(2,1)}, bf16[2,128,1536]{2,1,0:T(8,128)(2,1)}, bf16[256,3072]{1,0:T(8,128)(2,1)}) custom-call(bf16[1,256,2,4096]{3,2,1,0:T(2,128)(2,1)} %raw.3), custom_call_target="tpu_custom_call" | custom-call | bytes 4718592 | tf_op jit(solution)/shard_map/split/pallas_call | solution.py:143
  20.8 1.9 %collective-permute-start.4 = (bf16[2,128,1536]{2,1,0:T(8,128)(2,1)}, bf16[2,128,1536]{2,1,0:T(8,128)(2,1)}, u32[]{:S(2)}, u32[]{:S(2)}) collective-permute-start(bf16[2,128,1536]{2,1,0:T(8,128)(2,1)} %get-tuple-element.46), channel_id=1, source_target_pairs={{0,16},{16,32},{32,48},{48,64},{64,80},{80,96},{96,112},{112,128},... | collective-permute-start | bytes 2359304 | tf_op jit(solution)/shard_map/ppermute | solution.py:386
  22.7 6.0 %collective-permute-start.5 = (bf16[2,128,1536]{2,1,0:T(8,128)(2,1)}, bf16[2,128,1536]{2,1,0:T(8,128)(2,1)}, u32[]{:S(2)}, u32[]{:S(2)}) collective-permute-start(bf16[2,128,1536]{2,1,0:T(8,128)(2,1)} %get-tuple-element.45), channel_id=1, source_target_pairs={{16,0},{32,16},{48,32},{64,48},{80,64},{96,80},{112,96},{128,112},... | collective-permute-start | bytes 2359304 | tf_op jit(solution)/shard_map/ppermute | solution.py:386
  28.8 0.5 fusion.2
  29.4 0.1 maximum_maximum_fusion.table_ref
  29.5 3.8 %split.5 = (bf16[2,128,1024]{2,1,0:T(8,128)(2,1)}, bf16[2,128,1024]{2,1,0:T(8,128)(2,1)}, bf16[256,2048]{1,0:T(8,128)(2,1)}) custom-call(bf16[1,256,2,4096]{3,2,1,0:T(2,128)(2,1)} %raw.3), custom_call_target="tpu_custom_call" | custom-call | bytes 3145728 | tf_op jit(solution)/shard_map/split/pallas_call | solution.py:143
  34.0 0.1 copy.5
  34.0 0.1 reshape.56
  34.2 3.0 %white.1.white_ref = bf16[256,3072]{1,0:T(8,128)(2,1)S(1)} custom-call(bf16[2,128,1536]{2,1,0:T(8,128)(2,1)} %get-tuple-element.52.first, bf16[2,128,1536]{2,1,0:T(8,128)(2,1)} %get-tuple-element.53.second), custom_call_target="tpu_custom_call" | custom-call | bytes 3145728 | tf_op jit(solution)/shard_map/white/pallas_call | solution.py:157
  37.2 6.1 %early_pairs.2.refs_0_ = f32[1792,256]{1,0:T(8,128)} custom-call(bf16[2,128,1536]{2,1,0:T(8,128)(2,1)} %copy-done.3, bf16[2,128,1536]{2,1,0:T(8,128)(2,1)} %copy-done.4, f32[8,4096]{1,0:T(8,128)S(1)} %maximum_maximum_fusion.table_ref, bf16[256,3072]{1,0:T(8,128)(2,1)S(1)} %white.1.white_ref), custom_call_target="tpu_custom_call" | custom-call | flops 2818572288 | bytes 8388608 | tf_op jit(solution)/shard_map/early_pairs/pallas_call | solution.py:325
  43.3 1.9 %collective-permute-start.2 = (bf16[2,128,1024]{2,1,0:T(8,128)(2,1)}, bf16[2,128,1024]{2,1,0:T(8,128)(2,1)S(1)}, u32[]{:S(2)}, u32[]{:S(2)}) collective-permute-start(bf16[2,128,1024]{2,1,0:T(8,128)(2,1)} %get-tuple-element.54), channel_id=1, source_target_pairs={{0,16},{16,32},{32,48},{48,64},{64,80},{80,96},{96,112},{112,128},... | collective-permute-start | bytes 1572872 | tf_op jit(solution)/shard_map/ppermute | solution.py:386
  45.2 6.1 %collective-permute-start.3 = (bf16[2,128,1024]{2,1,0:T(8,128)(2,1)}, bf16[2,128,1024]{2,1,0:T(8,128)(2,1)}, u32[]{:S(2)}, u32[]{:S(2)}) collective-permute-start(bf16[2,128,1024]{2,1,0:T(8,128)(2,1)} %get-tuple-element.55), channel_id=1, source_target_pairs={{16,0},{32,16},{48,32},{64,48},{80,64},{96,80},{112,96},{128,112},... | collective-permute-start | bytes 1572872 | tf_op jit(solution)/shard_map/ppermute | solution.py:386
  51.4 0.6 bitcast_and_fusion.2
  52.7 0.1 conditional.1
  52.8 7.0 %early_pairs.3.before = f32[1792,256]{1,0:T(8,128)} custom-call(bf16[2,128,1536]{2,1,0:T(8,128)(2,1)} %collective-permute-done.4.left, bf16[2,128,1536]{2,1,0:T(8,128)(2,1)} %collective-permute-done.5.right, f32[8,4096]{1,0:T(8,128)S(1)} %maximum_maximum_fusion.table_ref, bf16[256,3072]{1,0:T(8,128)(2,1)} %get-tuple-element.57.white_ref, ...), custom_call_target="tpu_custom_call" | custom-call | flops 2818572288 | bytes 8388608 | tf_op jit(solution)/shard_map/early_pairs/pallas_call | solution.py:325
  59.8 0.5 collective-permute-done.2.left
  60.3 1.3 %collective-permute-done.3.right = bf16[2,128,1024]{2,1,0:T(8,128)(2,1)} collective-permute-done((bf16[2,128,1024]{2,1,0:T(8,128)(2,1)}, bf16[2,128,1024]{2,1,0:T(8,128)(2,1)}, u32[]{:S(2)}, u32[]{:S(2)}) %collective-permute-start.3) | collective-permute-done | bytes 524320 | tf_op jit(solution)/shard_map/ppermute | solution.py:386
  61.6 6.1 %last_pairs.1 = (f32[8,240,128]{2,1,0:T(8,128)}, bf16[8,240,128]{2,1,0:T(8,128)(2,1)}) custom-call(s32[7]{0:T(128)S(1)} %pad_add_fusion.slots, bf16[2,128,1024]{2,1,0:T(8,128)(2,1)} %copy-done.5, bf16[2,128,1024]{2,1,0:T(8,128)(2,1)} %collective-permute-done.3.right, f32[8,4096]{1,0:T(8,128)S(1)} %maximum_maximum_fusion.table_ref, ...), custom_call_target="tpu_custom_call" | custom-call | flops 1879048192 | bytes 8388608 | tf_op jit(solution)/shard_map/last_pairs/pallas_call | solution.py:349
  67.8 2.1 %collective-permute-start.6 = (bf16[8,240,128]{2,1,0:T(8,128)(2,1)}, bf16[8,240,128]{2,1,0:T(8,128)(2,1)S(1)}, u32[]{:S(2)}, u32[]{:S(2)}) collective-permute-start(bf16[8,240,128]{2,1,0:T(8,128)(2,1)} %get-tuple-element.60), channel_id=1, source_target_pairs={{0,1},{1,0},{2,3},{3,2},{4,5},{5,4},{6,7},{7,6},{8,9},{9,8},{10,11... | collective-permute-start | bytes 1474568 | tf_op jit(solution)/shard_map/ppermute | solution.py:421
  69.9 2.0 %collective-permute-done.6 = bf16[8,240,128]{2,1,0:T(8,128)(2,1)S(1)} collective-permute-done((bf16[8,240,128]{2,1,0:T(8,128)(2,1)}, bf16[8,240,128]{2,1,0:T(8,128)(2,1)S(1)}, u32[]{:S(2)}, u32[]{:S(2)}) %collective-permute-start.6) | collective-permute-done | bytes 491552 | tf_op jit(solution)/shard_map/ppermute | solution.py:421
  71.9 1.0 %add_convert_fusion.1 = bf16[8,96,128]{2,1,0:T(8,128)(2,1)S(1)} fusion(f32[8,240,128]{2,1,0:T(8,128)} %get-tuple-element.59, bf16[8,240,128]{2,1,0:T(8,128)(2,1)S(1)} %collective-permute-done.6), kind=kLoop, calls=%fused_computation.2 | loop fusion | flops 294912 | bytes 786432 | tf_op jit(solution)/shard_map/convert_element_type | solution.py:426
  73.0 1.9 %collective-permute-start.7 = (bf16[8,48,128]{2,1,0:T(8,128)(2,1)S(1)}, bf16[8,48,128]{2,1,0:T(8,128)(2,1)S(1)}, u32[]{:S(2)}, u32[]{:S(2)}) collective-permute-start(bf16[8,48,128]{2,1,0:T(8,128)(2,1)S(1)} %get-tuple-element.61), channel_id=1, source_target_pairs={{0,16},{16,0},{32,48},{48,32},{64,80},{80,64},{96,112},{112,96},{1... | collective-permute-start | bytes 294920 | tf_op jit(solution)/shard_map/ppermute | solution.py:431
  74.9 6.5 %collective-permute-start.8 = (bf16[8,48,128]{2,1,0:T(8,128)(2,1)S(1)}, bf16[8,48,128]{2,1,0:T(8,128)(2,1)S(1)}, u32[]{:S(2)}, u32[]{:S(2)}) collective-permute-start(bf16[8,48,128]{2,1,0:T(8,128)(2,1)S(1)} %get-tuple-element.62), channel_id=1, source_target_pairs={{16,32},{32,16},{48,64},{64,48},{80,96},{96,80},{112,128},{128,112... | collective-permute-start | bytes 294920 | tf_op jit(solution)/shard_map/ppermute | solution.py:432
  81.5 0.1 broadcast_in_dim.57
  81.7 0.1 broadcast_in_dim.54
  81.8 2.7 %collective-permute-done.8 = bf16[8,48,128]{2,1,0:T(8,128)(2,1)S(1)} collective-permute-done((bf16[8,48,128]{2,1,0:T(8,128)(2,1)S(1)}, bf16[8,48,128]{2,1,0:T(8,128)(2,1)S(1)}, u32[]{:S(2)}, u32[]{:S(2)}) %collective-permute-start.8) | collective-permute-done | bytes 98336 | tf_op jit(solution)/shard_map/ppermute | solution.py:432
  84.5 0.2 fusion
  84.7 19.3 %all_to_all.5 = bf16[8,144,128]{2,1,0:T(8,128)(2,1)S(1)} all-to-all(bf16[8,144,128]{2,1,0:T(8,128)(2,1)S(1)} %fusion), channel_id=1, replica_groups=mesh['sta'=32,'seg'=8,'band'=2] {'seg'}, dimensions={0} | all-to-all | bytes 589824 | tf_op jit(solution)/shard_map/all_to_all | solution.py:437
  104.0 0.6 broadcast_multiply_fusion
  (28 shorter events, 0.5 us)
Async XLA Ops:
  2.6 31.5 %collective-permute-start = (bf16[2,128,1536]{2,1,0:T(8,128)(2,1)}, bf16[2,128,1536]{2,1,0:T(8,128)(2,1)S(1)}, u32[]{:S(2)}, u32[]{:S(2)}) collective-permute-start(bf16[2,128,1536]{2,1,0:T(8,128)(2,1)} %get-tuple-element.53.second), channel_id=1, source_target_pairs={{0,16},{16,32},{32,48},{48,64},{64,80},{80,96},{96,112},{112,128},... | collective-permute-start | bytes 2359304 | tf_op jit(solution)/shard_map/ppermute | solution.py:386
  6.9 27.2 %collective-permute-start.1 = (bf16[2,128,1536]{2,1,0:T(8,128)(2,1)}, bf16[2,128,1536]{2,1,0:T(8,128)(2,1)S(1)}, u32[]{:S(2)}, u32[]{:S(2)}) collective-permute-start(bf16[2,128,1536]{2,1,0:T(8,128)(2,1)} %get-tuple-element.52.first), channel_id=1, source_target_pairs={{16,0},{32,16},{48,32},{64,48},{80,64},{96,80},{112,96},{128,112},... | collective-permute-start | bytes 2359304 | tf_op jit(solution)/shard_map/ppermute | solution.py:386
  20.8 32.0 %collective-permute-start.4 = (bf16[2,128,1536]{2,1,0:T(8,128)(2,1)}, bf16[2,128,1536]{2,1,0:T(8,128)(2,1)}, u32[]{:S(2)}, u32[]{:S(2)}) collective-permute-start(bf16[2,128,1536]{2,1,0:T(8,128)(2,1)} %get-tuple-element.46), channel_id=1, source_target_pairs={{0,16},{16,32},{32,48},{48,64},{64,80},{80,96},{96,112},{112,128},... | collective-permute-start | bytes 2359304 | tf_op jit(solution)/shard_map/ppermute | solution.py:386
  22.7 30.1 %collective-permute-start.5 = (bf16[2,128,1536]{2,1,0:T(8,128)(2,1)}, bf16[2,128,1536]{2,1,0:T(8,128)(2,1)}, u32[]{:S(2)}, u32[]{:S(2)}) collective-permute-start(bf16[2,128,1536]{2,1,0:T(8,128)(2,1)} %get-tuple-element.45), channel_id=1, source_target_pairs={{16,0},{32,16},{48,32},{64,48},{80,64},{96,80},{112,96},{128,112},... | collective-permute-start | bytes 2359304 | tf_op jit(solution)/shard_map/ppermute | solution.py:386
  29.5 4.4 %copy-start.1 = (s32[3,2]{0,1:T(2,128)S(1)}, s32[3,2]{0,1:T(2,128)}, u32[]{:S(2)}) copy-start(s32[3,2]{0,1:T(2,128)} %param.6) | copy-start | bytes 76
  34.1 3.0 %copy-start.3 = (bf16[2,128,1536]{2,1,0:T(8,128)(2,1)}, bf16[2,128,1536]{2,1,0:T(8,128)(2,1)S(1)}, u32[]{:S(2)}) copy-start(bf16[2,128,1536]{2,1,0:T(8,128)(2,1)S(1)} %collective-permute-done.left) | copy-start | bytes 2359300
  34.1 3.1 %copy-start.4 = (bf16[2,128,1536]{2,1,0:T(8,128)(2,1)}, bf16[2,128,1536]{2,1,0:T(8,128)(2,1)S(1)}, u32[]{:S(2)}) copy-start(bf16[2,128,1536]{2,1,0:T(8,128)(2,1)S(1)} %collective-permute-done.1.right) | copy-start | bytes 2359300
  43.3 17.0 %collective-permute-start.2 = (bf16[2,128,1024]{2,1,0:T(8,128)(2,1)}, bf16[2,128,1024]{2,1,0:T(8,128)(2,1)S(1)}, u32[]{:S(2)}, u32[]{:S(2)}) collective-permute-start(bf16[2,128,1024]{2,1,0:T(8,128)(2,1)} %get-tuple-element.54), channel_id=1, source_target_pairs={{0,16},{16,32},{32,48},{48,64},{64,80},{80,96},{96,112},{112,128},... | collective-permute-start | bytes 1572872 | tf_op jit(solution)/shard_map/ppermute | solution.py:386
  45.2 16.4 %collective-permute-start.3 = (bf16[2,128,1024]{2,1,0:T(8,128)(2,1)}, bf16[2,128,1024]{2,1,0:T(8,128)(2,1)}, u32[]{:S(2)}, u32[]{:S(2)}) collective-permute-start(bf16[2,128,1024]{2,1,0:T(8,128)(2,1)} %get-tuple-element.55), channel_id=1, source_target_pairs={{16,0},{32,16},{48,32},{64,48},{80,64},{96,80},{112,96},{128,112},... | collective-permute-start | bytes 1572872 | tf_op jit(solution)/shard_map/ppermute | solution.py:386
  52.8 8.8 %copy-start.2 = (bf16[256,2048]{1,0:T(8,128)(2,1)S(1)}, bf16[256,2048]{1,0:T(8,128)(2,1)}, u32[]{:S(2)}) copy-start(bf16[256,2048]{1,0:T(8,128)(2,1)} %get-tuple-element.56.white_ref) | copy-start | bytes 3145732
  60.3 1.3 %copy-start.5 = (bf16[2,128,1024]{2,1,0:T(8,128)(2,1)}, bf16[2,128,1024]{2,1,0:T(8,128)(2,1)S(1)}, u32[]{:S(2)}) copy-start(bf16[2,128,1024]{2,1,0:T(8,128)(2,1)S(1)} %collective-permute-done.2.left) | copy-start | bytes 1572868
  67.8 16.7 %copy-start = (f32[8,240,128]{2,1,0:T(8,128)S(1)}, f32[8,240,128]{2,1,0:T(8,128)}, u32[]{:S(2)}) copy-start(f32[8,240,128]{2,1,0:T(8,128)} %get-tuple-element.59) | copy-start | bytes 2949124
  67.8 4.1 %collective-permute-start.6 = (bf16[8,240,128]{2,1,0:T(8,128)(2,1)}, bf16[8,240,128]{2,1,0:T(8,128)(2,1)S(1)}, u32[]{:S(2)}, u32[]{:S(2)}) collective-permute-start(bf16[8,240,128]{2,1,0:T(8,128)(2,1)} %get-tuple-element.60), channel_id=1, source_target_pairs={{0,1},{1,0},{2,3},{3,2},{4,5},{5,4},{6,7},{7,6},{8,9},{9,8},{10,11... | collective-permute-start | bytes 1474568 | tf_op jit(solution)/shard_map/ppermute | solution.py:421
  73.0 8.8 %collective-permute-start.7 = (bf16[8,48,128]{2,1,0:T(8,128)(2,1)S(1)}, bf16[8,48,128]{2,1,0:T(8,128)(2,1)S(1)}, u32[]{:S(2)}, u32[]{:S(2)}) collective-permute-start(bf16[8,48,128]{2,1,0:T(8,128)(2,1)S(1)} %get-tuple-element.61), channel_id=1, source_target_pairs={{0,16},{16,0},{32,48},{48,32},{64,80},{80,64},{96,112},{112,96},{1... | collective-permute-start | bytes 294920 | tf_op jit(solution)/shard_map/ppermute | solution.py:431
  74.9 9.6 %collective-permute-start.8 = (bf16[8,48,128]{2,1,0:T(8,128)(2,1)S(1)}, bf16[8,48,128]{2,1,0:T(8,128)(2,1)S(1)}, u32[]{:S(2)}, u32[]{:S(2)}) collective-permute-start(bf16[8,48,128]{2,1,0:T(8,128)(2,1)S(1)} %get-tuple-element.62), channel_id=1, source_target_pairs={{16,32},{32,16},{48,64},{64,48},{80,96},{96,80},{112,128},{128,112... | collective-permute-start | bytes 294920 | tf_op jit(solution)/shard_map/ppermute | solution.py:432

commit v6 on v5

--- a/solution.py
+++ b/solution.py
@@ -294,7 +294,7 @@
             even = jnp.concatenate([o[:, 0] for o in octets], axis=1)
             odd = jnp.concatenate([o[:, 1] for o in octets], axis=1)
             rows = pl.ds(place * 8 if isinstance(place, int) else pl.multiple_of(place * 8, 16), 16)
-            keep_ref[:, rows, :] = jnp.where(even_core, even, odd)
+            keep_ref[:, rows, :] = jnp.where(even_core, even, odd).astype(jnp.bfloat16)
             send_ref[:, rows, :] = jnp.where(even_core, odd, even).astype(jnp.bfloat16)
 
         for slot in range(PAIR_CAP):
@@ -348,7 +348,7 @@
     there = pl.BlockSpec(memory_space=pl.ANY)
     return pl.pallas_call(
         last_kernel,
-        out_shape=(jax.ShapeDtypeStruct(result, jnp.float32), jax.ShapeDtypeStruct(result, jnp.bfloat16)),
+        out_shape=(jax.ShapeDtypeStruct(result, jnp.bfloat16),) * 2,
         grid_spec=pltpu.PrefetchScalarGridSpec(
             num_scalar_prefetch=1,
             grid=(bins // STEP,),
@@ -423,7 +423,7 @@
 
     def summed(start, count):
         rows = slice(start, start + count)
-        return (keep[:, rows] + other[:, rows].astype(jnp.float32)).astype(jnp.bfloat16)
+        return (keep[:, rows].astype(jnp.float32) + other[:, rows].astype(jnp.float32)).astype(jnp.bfloat16)
 
     swap_even = [(i, i ^ 1) for i in range(sta_count)]
     swap_odd = [(i, ((i + 1) ^ 1) - 1) for i in range(1, sta_count - 1)]

time: 105 us -> 106 us (level)
  no operation moved by 1% of the time
where the time goes in v6:
time: 106 us; the launch traced here: 105 us
  starting transfers between devices  39.4 us (37%)
  Pallas kernels  33.6 us (32%)
  blocking collectives  19.3 us (18%)
  waiting for transfers between devices  6.5 us (6%)
  other arithmetic  4.27 us (4%)
  between operations  1.54 us (1%)
    ppermute x3, starting transfers between devices, send(): lax.ppermute(pair[0], 'sta', to_left)  21 us
    all_to_all x1, blocking collectives, body(): gathered = lax.all_to_all(pieces.reshape(8, own_rows, STA), 'seg', 0, 0)  19.3 us
    pallas_call x2, Pallas kernels, early_part(): pl.pallas_call(early_kernel, out_shape=jax.ShapeDtypeStruct(SUMS, jnp.flo...  13.1 us
    pallas_call x3, Pallas kernels, split(): pl.pallas_call(split_kernel, out_shape=(shape, shape) + (white_shape(coun...  11.5 us
    ppermute x3, starting transfers between devices, send(): lax.ppermute(pair[1], 'sta', to_right)  8.09 us
    ppermute x1, starting transfers between devices, body(): got_odd = lax.ppermute(foreign[:, LAGS * 8:], 'sta', swap_odd)  6.5 us
    pallas_call x1, Pallas kernels, last_part(): pl.pallas_call(last_kernel, out_shape=(jax.ShapeDtypeStruct(result, jnp.b...  5.94 us
    pallas_call x1, Pallas kernels, white_part(): pl.pallas_call(white_kernel, out_shape=white_shape(count), grid=(count //...  3.02 us
  transfers between devices with their start and end apart: 9, of which 4 were waited for; matrix products, arithmetic and copies ran while one was open for 2% of the time, Pallas kernels for 24%

profile of v6, /device:TPU:6, one launch (start us, length us, event | category | flops | bytes accessed | tf_op | source)
XLA Modules:
  0.0 105.2 jit_solution(10504159102980719334)
XLA Ops:
  0.0 2.6 %split.3 = (bf16[2,128,1536]{2,1,0:T(8,128)(2,1)}, bf16[2,128,1536]{2,1,0:T(8,128)(2,1)}) custom-call(bf16[1,256,2,4096]{3,2,1,0:T(2,128)(2,1)} %raw.3), custom_call_target="tpu_custom_call" | custom-call | bytes 4718592 | tf_op jit(solution)/shard_map/split/pallas_call | solution.py:143
  2.6 4.3 %collective-permute-start = (bf16[2,128,1536]{2,1,0:T(8,128)(2,1)}, bf16[2,128,1536]{2,1,0:T(8,128)(2,1)S(1)}, u32[]{:S(2)}, u32[]{:S(2)}) collective-permute-start(bf16[2,128,1536]{2,1,0:T(8,128)(2,1)} %get-tuple-element.53.second), channel_id=1, source_target_pairs={{0,16},{16,32},{32,48},{48,64},{64,80},{80,96},{96,112},{112,128},... | collective-permute-start | bytes 2359304 | tf_op jit(solution)/shard_map/ppermute | solution.py:386
  6.9 8.9 %collective-permute-start.1 = (bf16[2,128,1536]{2,1,0:T(8,128)(2,1)}, bf16[2,128,1536]{2,1,0:T(8,128)(2,1)S(1)}, u32[]{:S(2)}, u32[]{:S(2)}) collective-permute-start(bf16[2,128,1536]{2,1,0:T(8,128)(2,1)} %get-tuple-element.52.first), channel_id=1, source_target_pairs={{16,0},{32,16},{48,32},{64,48},{80,64},{96,80},{112,96},{128,112},... | collective-permute-start | bytes 2359304 | tf_op jit(solution)/shard_map/ppermute | solution.py:386
  15.8 5.0 %split.4 = (bf16[2,128,1536]{2,1,0:T(8,128)(2,1)}, bf16[2,128,1536]{2,1,0:T(8,128)(2,1)}, bf16[256,3072]{1,0:T(8,128)(2,1)}) custom-call(bf16[1,256,2,4096]{3,2,1,0:T(2,128)(2,1)} %raw.3), custom_call_target="tpu_custom_call" | custom-call | bytes 4718592 | tf_op jit(solution)/shard_map/split/pallas_call | solution.py:143
  20.8 1.9 %collective-permute-start.4 = (bf16[2,128,1536]{2,1,0:T(8,128)(2,1)}, bf16[2,128,1536]{2,1,0:T(8,128)(2,1)}, u32[]{:S(2)}, u32[]{:S(2)}) collective-permute-start(bf16[2,128,1536]{2,1,0:T(8,128)(2,1)} %get-tuple-element.46), channel_id=1, source_target_pairs={{0,16},{16,32},{32,48},{48,64},{64,80},{80,96},{96,112},{112,128},... | collective-permute-start | bytes 2359304 | tf_op jit(solution)/shard_map/ppermute | solution.py:386
  22.7 6.0 %collective-permute-start.5 = (bf16[2,128,1536]{2,1,0:T(8,128)(2,1)}, bf16[2,128,1536]{2,1,0:T(8,128)(2,1)}, u32[]{:S(2)}, u32[]{:S(2)}) collective-permute-start(bf16[2,128,1536]{2,1,0:T(8,128)(2,1)} %get-tuple-element.45), channel_id=1, source_target_pairs={{16,0},{32,16},{48,32},{64,48},{80,64},{96,80},{112,96},{128,112},... | collective-permute-start | bytes 2359304 | tf_op jit(solution)/shard_map/ppermute | solution.py:386
  28.8 0.5 fusion.2
  29.4 0.1 maximum_maximum_fusion.table_ref
  29.5 3.8 %split.5 = (bf16[2,128,1024]{2,1,0:T(8,128)(2,1)}, bf16[2,128,1024]{2,1,0:T(8,128)(2,1)}, bf16[256,2048]{1,0:T(8,128)(2,1)}) custom-call(bf16[1,256,2,4096]{3,2,1,0:T(2,128)(2,1)} %raw.3), custom_call_target="tpu_custom_call" | custom-call | bytes 3145728 | tf_op jit(solution)/shard_map/split/pallas_call | solution.py:143
  34.0 0.1 copy.5
  34.1 0.1 reshape.56
  34.2 3.0 %white.1.white_ref = bf16[256,3072]{1,0:T(8,128)(2,1)S(1)} custom-call(bf16[2,128,1536]{2,1,0:T(8,128)(2,1)} %get-tuple-element.52.first, bf16[2,128,1536]{2,1,0:T(8,128)(2,1)} %get-tuple-element.53.second), custom_call_target="tpu_custom_call" | custom-call | bytes 3145728 | tf_op jit(solution)/shard_map/white/pallas_call | solution.py:157
  37.2 6.1 %early_pairs.2.refs_0_ = f32[1792,256]{1,0:T(8,128)} custom-call(bf16[2,128,1536]{2,1,0:T(8,128)(2,1)} %copy-done.2, bf16[2,128,1536]{2,1,0:T(8,128)(2,1)} %copy-done.3, f32[8,4096]{1,0:T(8,128)S(1)} %maximum_maximum_fusion.table_ref, bf16[256,3072]{1,0:T(8,128)(2,1)S(1)} %white.1.white_ref), custom_call_target="tpu_custom_call" | custom-call | flops 2818572288 | bytes 8388608 | tf_op jit(solution)/shard_map/early_pairs/pallas_call | solution.py:325
  43.3 1.9 %collective-permute-start.2 = (bf16[2,128,1024]{2,1,0:T(8,128)(2,1)}, bf16[2,128,1024]{2,1,0:T(8,128)(2,1)S(1)}, u32[]{:S(2)}, u32[]{:S(2)}) collective-permute-start(bf16[2,128,1024]{2,1,0:T(8,128)(2,1)} %get-tuple-element.54), channel_id=1, source_target_pairs={{0,16},{16,32},{32,48},{48,64},{64,80},{80,96},{96,112},{112,128},... | collective-permute-start | bytes 1572872 | tf_op jit(solution)/shard_map/ppermute | solution.py:386
  45.3 6.1 %collective-permute-start.3 = (bf16[2,128,1024]{2,1,0:T(8,128)(2,1)}, bf16[2,128,1024]{2,1,0:T(8,128)(2,1)}, u32[]{:S(2)}, u32[]{:S(2)}) collective-permute-start(bf16[2,128,1024]{2,1,0:T(8,128)(2,1)} %get-tuple-element.55), channel_id=1, source_target_pairs={{16,0},{32,16},{48,32},{64,48},{80,64},{96,80},{112,96},{128,112},... | collective-permute-start | bytes 1572872 | tf_op jit(solution)/shard_map/ppermute | solution.py:386
  51.4 0.7 bitcast_and_fusion.2
  52.8 0.1 conditional.1
  52.9 7.0 %early_pairs.3.before = f32[1792,256]{1,0:T(8,128)} custom-call(bf16[2,128,1536]{2,1,0:T(8,128)(2,1)} %collective-permute-done.4.left, bf16[2,128,1536]{2,1,0:T(8,128)(2,1)} %collective-permute-done.5.right, f32[8,4096]{1,0:T(8,128)S(1)} %maximum_maximum_fusion.table_ref, bf16[256,3072]{1,0:T(8,128)(2,1)} %get-tuple-element.57.white_ref, ...), custom_call_target="tpu_custom_call" | custom-call | flops 2818572288 | bytes 8388608 | tf_op jit(solution)/shard_map/early_pairs/pallas_call | solution.py:325
  59.9 0.4 collective-permute-done.2.left
  60.4 1.3 %collective-permute-done.3.right = bf16[2,128,1024]{2,1,0:T(8,128)(2,1)} collective-permute-done((bf16[2,128,1024]{2,1,0:T(8,128)(2,1)}, bf16[2,128,1024]{2,1,0:T(8,128)(2,1)}, u32[]{:S(2)}, u32[]{:S(2)}) %collective-permute-start.3) | collective-permute-done | bytes 524320 | tf_op jit(solution)/shard_map/ppermute | solution.py:386
  61.7 5.9 %last_pairs.1 = (bf16[8,240,128]{2,1,0:T(8,128)(2,1)}, bf16[8,240,128]{2,1,0:T(8,128)(2,1)}) custom-call(s32[7]{0:T(128)S(1)} %pad_add_fusion.slots, bf16[2,128,1024]{2,1,0:T(8,128)(2,1)} %copy-done.4, bf16[2,128,1024]{2,1,0:T(8,128)(2,1)} %collective-permute-done.3.right, f32[8,4096]{1,0:T(8,128)S(1)} %maximum_maximum_fusion.table_ref, ...), custom_call_target="tpu_custom_call" | custom-call | flops 1879048192 | bytes 8388608 | tf_op jit(solution)/shard_map/last_pairs/pallas_call | solution.py:349
  67.6 1.9 %collective-permute-start.6 = (bf16[8,240,128]{2,1,0:T(8,128)(2,1)}, bf16[8,240,128]{2,1,0:T(8,128)(2,1)S(1)}, u32[]{:S(2)}, u32[]{:S(2)}) collective-permute-start(bf16[8,240,128]{2,1,0:T(8,128)(2,1)} %get-tuple-element.60), channel_id=1, source_target_pairs={{0,1},{1,0},{2,3},{3,2},{4,5},{5,4},{6,7},{7,6},{8,9},{9,8},{10,11... | collective-permute-start | bytes 1474568 | tf_op jit(solution)/shard_map/ppermute | solution.py:421
  69.5 2.0 %collective-permute-done.6 = bf16[8,240,128]{2,1,0:T(8,128)(2,1)S(1)} collective-permute-done((bf16[8,240,128]{2,1,0:T(8,128)(2,1)}, bf16[8,240,128]{2,1,0:T(8,128)(2,1)S(1)}, u32[]{:S(2)}, u32[]{:S(2)}) %collective-permute-start.6) | collective-permute-done | bytes 491552 | tf_op jit(solution)/shard_map/ppermute | solution.py:421
  71.6 1.0 add_convert_fusion.1
  72.6 1.9 %collective-permute-start.7 = (bf16[8,48,128]{2,1,0:T(8,128)(2,1)S(1)}, bf16[8,48,128]{2,1,0:T(8,128)(2,1)S(1)}, u32[]{:S(2)}, u32[]{:S(2)}) collective-permute-start(bf16[8,48,128]{2,1,0:T(8,128)(2,1)S(1)} %get-tuple-element.61), channel_id=1, source_target_pairs={{0,16},{16,0},{32,48},{48,32},{64,80},{80,64},{96,112},{112,96},{1... | collective-permute-start | bytes 294920 | tf_op jit(solution)/shard_map/ppermute | solution.py:431
  74.5 6.5 %collective-permute-start.8 = (bf16[8,48,128]{2,1,0:T(8,128)(2,1)S(1)}, bf16[8,48,128]{2,1,0:T(8,128)(2,1)S(1)}, u32[]{:S(2)}, u32[]{:S(2)}) collective-permute-start(bf16[8,48,128]{2,1,0:T(8,128)(2,1)S(1)} %get-tuple-element.62), channel_id=1, source_target_pairs={{16,32},{32,16},{48,64},{64,48},{80,96},{96,80},{112,128},{128,112... | collective-permute-start | bytes 294920 | tf_op jit(solution)/shard_map/ppermute | solution.py:432
  81.1 0.1 broadcast_in_dim.57
  81.3 0.1 broadcast_in_dim.54
  81.4 2.7 %collective-permute-done.8 = bf16[8,48,128]{2,1,0:T(8,128)(2,1)S(1)} collective-permute-done((bf16[8,48,128]{2,1,0:T(8,128)(2,1)S(1)}, bf16[8,48,128]{2,1,0:T(8,128)(2,1)S(1)}, u32[]{:S(2)}, u32[]{:S(2)}) %collective-permute-start.8) | collective-permute-done | bytes 98336 | tf_op jit(solution)/shard_map/ppermute | solution.py:432
  84.1 1.2 %fusion = bf16[8,144,128]{2,1,0:T(8,128)(2,1)S(1)} fusion(bf16[8,240,128]{2,1,0:T(8,128)(2,1)S(1)} %collective-permute-done.6, bf16[8,240,128]{2,1,0:T(8,128)(2,1)} %get-tuple-element.59, pred[144]{0:T(512)(128)(4,1)S(1)} %broadcast_in_dim.57, pred[144]{0:T(512)(128)(4,1)S(1)} %broadcast_in_dim.54, bf16[8,48,128]{2,1,0:T(8,128)(2,1)S(1)} %collective-permute-done.8, ...), kind=kLoop, calls=%fused_computation.3 | loop fusion | flops 884736 | bytes 1081632 | tf_op jit(solution)/shard_map/jit(_where)/select_n | solution.py:436
  85.3 19.3 %all_to_all.5 = bf16[8,144,128]{2,1,0:T(8,128)(2,1)S(1)} all-to-all(bf16[8,144,128]{2,1,0:T(8,128)(2,1)S(1)} %fusion), channel_id=1, replica_groups=mesh['sta'=32,'seg'=8,'band'=2] {'seg'}, dimensions={0} | all-to-all | bytes 589824 | tf_op jit(solution)/shard_map/all_to_all | solution.py:437
  104.6 0.6 broadcast_multiply_fusion
  (26 shorter events, 0.5 us)
Async XLA Ops:
  2.6 31.5 %collective-permute-start = (bf16[2,128,1536]{2,1,0:T(8,128)(2,1)}, bf16[2,128,1536]{2,1,0:T(8,128)(2,1)S(1)}, u32[]{:S(2)}, u32[]{:S(2)}) collective-permute-start(bf16[2,128,1536]{2,1,0:T(8,128)(2,1)} %get-tuple-element.53.second), channel_id=1, source_target_pairs={{0,16},{16,32},{32,48},{48,64},{64,80},{80,96},{96,112},{112,128},... | collective-permute-start | bytes 2359304 | tf_op jit(solution)/shard_map/ppermute | solution.py:386
  6.9 27.3 %collective-permute-start.1 = (bf16[2,128,1536]{2,1,0:T(8,128)(2,1)}, bf16[2,128,1536]{2,1,0:T(8,128)(2,1)S(1)}, u32[]{:S(2)}, u32[]{:S(2)}) collective-permute-start(bf16[2,128,1536]{2,1,0:T(8,128)(2,1)} %get-tuple-element.52.first), channel_id=1, source_target_pairs={{16,0},{32,16},{48,32},{64,48},{80,64},{96,80},{112,96},{128,112},... | collective-permute-start | bytes 2359304 | tf_op jit(solution)/shard_map/ppermute | solution.py:386
  20.8 32.1 %collective-permute-start.4 = (bf16[2,128,1536]{2,1,0:T(8,128)(2,1)}, bf16[2,128,1536]{2,1,0:T(8,128)(2,1)}, u32[]{:S(2)}, u32[]{:S(2)}) collective-permute-start(bf16[2,128,1536]{2,1,0:T(8,128)(2,1)} %get-tuple-element.46), channel_id=1, source_target_pairs={{0,16},{16,32},{32,48},{48,64},{64,80},{80,96},{96,112},{112,128},... | collective-permute-start | bytes 2359304 | tf_op jit(solution)/shard_map/ppermute | solution.py:386
  22.7 30.2 %collective-permute-start.5 = (bf16[2,128,1536]{2,1,0:T(8,128)(2,1)}, bf16[2,128,1536]{2,1,0:T(8,128)(2,1)}, u32[]{:S(2)}, u32[]{:S(2)}) collective-permute-start(bf16[2,128,1536]{2,1,0:T(8,128)(2,1)} %get-tuple-element.45), channel_id=1, source_target_pairs={{16,0},{32,16},{48,32},{64,48},{80,64},{96,80},{112,96},{128,112},... | collective-permute-start | bytes 2359304 | tf_op jit(solution)/shard_map/ppermute | solution.py:386
  29.5 4.5 %copy-start = (s32[3,2]{0,1:T(2,128)S(1)}, s32[3,2]{0,1:T(2,128)}, u32[]{:S(2)}) copy-start(s32[3,2]{0,1:T(2,128)} %param.6) | copy-start | bytes 76
  34.2 3.0 %copy-start.2 = (bf16[2,128,1536]{2,1,0:T(8,128)(2,1)}, bf16[2,128,1536]{2,1,0:T(8,128)(2,1)S(1)}, u32[]{:S(2)}) copy-start(bf16[2,128,1536]{2,1,0:T(8,128)(2,1)S(1)} %collective-permute-done.left) | copy-start | bytes 2359300
  34.2 3.1 %copy-start.3 = (bf16[2,128,1536]{2,1,0:T(8,128)(2,1)}, bf16[2,128,1536]{2,1,0:T(8,128)(2,1)S(1)}, u32[]{:S(2)}) copy-start(bf16[2,128,1536]{2,1,0:T(8,128)(2,1)S(1)} %collective-permute-done.1.right) | copy-start | bytes 2359300
  43.3 17.0 %collective-permute-start.2 = (bf16[2,128,1024]{2,1,0:T(8,128)(2,1)}, bf16[2,128,1024]{2,1,0:T(8,128)(2,1)S(1)}, u32[]{:S(2)}, u32[]{:S(2)}) collective-permute-start(bf16[2,128,1024]{2,1,0:T(8,128)(2,1)} %get-tuple-element.54), channel_id=1, source_target_pairs={{0,16},{16,32},{32,48},{48,64},{64,80},{80,96},{96,112},{112,128},... | collective-permute-start | bytes 1572872 | tf_op jit(solution)/shard_map/ppermute | solution.py:386
  45.3 16.4 %collective-permute-start.3 = (bf16[2,128,1024]{2,1,0:T(8,128)(2,1)}, bf16[2,128,1024]{2,1,0:T(8,128)(2,1)}, u32[]{:S(2)}, u32[]{:S(2)}) collective-permute-start(bf16[2,128,1024]{2,1,0:T(8,128)(2,1)} %get-tuple-element.55), channel_id=1, source_target_pairs={{16,0},{32,16},{48,32},{64,48},{80,64},{96,80},{112,96},{128,112},... | collective-permute-start | bytes 1572872 | tf_op jit(solution)/shard_map/ppermute | solution.py:386
  52.9 8.8 %copy-start.1 = (bf16[256,2048]{1,0:T(8,128)(2,1)S(1)}, bf16[256,2048]{1,0:T(8,128)(2,1)}, u32[]{:S(2)}) copy-start(bf16[256,2048]{1,0:T(8,128)(2,1)} %get-tuple-element.56.white_ref) | copy-start | bytes 3145732
  60.4 1.3 %copy-start.4 = (bf16[2,128,1024]{2,1,0:T(8,128)(2,1)}, bf16[2,128,1024]{2,1,0:T(8,128)(2,1)S(1)}, u32[]{:S(2)}) copy-start(bf16[2,128,1024]{2,1,0:T(8,128)(2,1)S(1)} %collective-permute-done.2.left) | copy-start | bytes 1572868
  67.6 4.0 %collective-permute-start.6 = (bf16[8,240,128]{2,1,0:T(8,128)(2,1)}, bf16[8,240,128]{2,1,0:T(8,128)(2,1)S(1)}, u32[]{:S(2)}, u32[]{:S(2)}) collective-permute-start(bf16[8,240,128]{2,1,0:T(8,128)(2,1)} %get-tuple-element.60), channel_id=1, source_target_pairs={{0,1},{1,0},{2,3},{3,2},{4,5},{5,4},{6,7},{7,6},{8,9},{9,8},{10,11... | collective-permute-start | bytes 1474568 | tf_op jit(solution)/shard_map/ppermute | solution.py:421
  72.6 8.8 %collective-permute-start.7 = (bf16[8,48,128]{2,1,0:T(8,128)(2,1)S(1)}, bf16[8,48,128]{2,1,0:T(8,128)(2,1)S(1)}, u32[]{:S(2)}, u32[]{:S(2)}) collective-permute-start(bf16[8,48,128]{2,1,0:T(8,128)(2,1)S(1)} %get-tuple-element.61), channel_id=1, source_target_pairs={{0,16},{16,0},{32,48},{48,32},{64,80},{80,64},{96,112},{112,96},{1... | collective-permute-start | bytes 294920 | tf_op jit(solution)/shard_map/ppermute | solution.py:431
  74.5 9.6 %collective-permute-start.8 = (bf16[8,48,128]{2,1,0:T(8,128)(2,1)S(1)}, bf16[8,48,128]{2,1,0:T(8,128)(2,1)S(1)}, u32[]{:S(2)}, u32[]{:S(2)}) collective-permute-start(bf16[8,48,128]{2,1,0:T(8,128)(2,1)S(1)} %get-tuple-element.62), channel_id=1, source_target_pairs={{16,32},{32,16},{48,64},{64,48},{80,96},{96,80},{112,128},{128,112... | collective-permute-start | bytes 294920 | tf_op jit(solution)/shard_map/ppermute | solution.py:432
